TPU v7x, 256 devices: a whole 4x4x8 slice. The times are simulated.
256 devices in a mesh: grp: 16 (over z_hi, y), resp: 16 (over z_lo, x, core).
Axes of the slice: x: 4, y: 4, z: 8 (z_hi: 4, z_lo: 2; z = z_hi * 2 + z_lo), core: 2. Of those that a mesh axis runs over, the one named last changes fastest.
Arguments:
- prompt_kv: bfloat16 [32768, 2, 512], P(('grp', 'resp')), parts along dimension 0, may hold values from -4 to 4
- queries: bfloat16 [32768, 2560], P(('grp', 'resp')), parts along dimension 0, may hold values from -100 to 100, as said below
- response_key_values: bfloat16 [32768, 2, 512], P(('grp', 'resp')), parts along dimension 0, may hold values from -4 to 4
- grad_out: bfloat16 [32768, 2560], P(('grp', 'resp')), parts along dimension 0, may hold values from -6 to 6
- lengths: int32 [256], P(('grp', 'resp')), parts along dimension 0, may hold values from 1 to 128, 1536 in all
Outputs:
- attn_out: bfloat16 [32768, 2560], P(('grp', 'resp')), parts along dimension 0
- grad_queries: bfloat16 [32768, 2560], P(('grp', 'resp')), parts along dimension 0
- grad_resp_kv: bfloat16 [32768, 2, 512], P(('grp', 'resp')), parts along dimension 0
- grad_prompt_kv: bfloat16 [32768, 2, 512], P(('grp', 'resp')), parts along dimension 0
There are 16 independent parts, one for each index of `grp`. A program takes and returns all parts, laid end to end along the dimension named above; each array names one. Nothing has to cross between parts.
Inputs may be any that keep to these rules, and one draw needn't show every extreme that they name: `lengths`: every response has at least one live token, and in each prompt's batch the longest response fills all 128 slots. `queries`: queries after their rotary position.
All inputs are finite; a program needn't handle non-finite values. No bound on the sum of `lengths` on one device may be relied on, other than what follows from the above.
Results may differ from a plain program's by a relative error of at most 0.024.
Values may be sent and summed in bfloat16 or wider, within the bound.
A program may use at most 128 MiB of HBM per device.

v0:
```python
import math

import jax
import jax.numpy as jnp
from jax import lax
from jax.sharding import PartitionSpec as P

HEAD_SIZE = 128


MASKED_SCORE = -1e30


def head_scores(head_query, head_keys):
    scores = jnp.einsum("rgd,ld->grl", head_query, head_keys, preferred_element_type=jnp.float32)
    return scores * (1.0 / math.sqrt(HEAD_SIZE))


def head_columns(key_value_head):
    return slice(key_value_head * HEAD_SIZE, (key_value_head + 1) * HEAD_SIZE)


def head_backward(weights, head_grad, head_values, row_delta):
    dweights = jnp.einsum("rgd,ld->grl", head_grad, head_values, preferred_element_type=jnp.float32)
    return (weights * (dweights - row_delta)).astype(jnp.bfloat16)


def per_device(prompt_kv, queries, response_key_values, grad_out, lengths):
    resp_len = queries.shape[0]
    key_value_width = response_key_values.shape[2]
    kv_heads = key_value_width // HEAD_SIZE
    group_width = queries.shape[1] // key_value_width
    prompt_len = prompt_kv.shape[0] * lax.axis_size("resp")
    inv_root = 1.0 / math.sqrt(HEAD_SIZE)
    query_heads = queries.reshape(resp_len, kv_heads, group_width, HEAD_SIZE)
    positions = jnp.arange(resp_len, dtype=jnp.int32)
    is_valid = positions < lengths[0]
    row_gradients = jnp.where(is_valid[:, None], grad_out, jnp.zeros_like(grad_out))
    head_gradients = row_gradients.reshape(resp_len, kv_heads, group_width, HEAD_SIZE)
    causal = positions[:, None] >= positions[None, :]
    gathered = lax.all_gather(prompt_kv, "resp", axis=0, tiled=True)
    visible = jnp.concatenate([jnp.full((resp_len, prompt_len), True), causal], axis=1)
    attended_list, query_list, key_list, value_list = ([], [], [], [])
    score_list, weight_list = ([], [])
    for key_value_head in range(kv_heads):
        columns = head_columns(key_value_head)
        head_keys = jnp.concatenate(
            [gathered[:, 0, columns], response_key_values[:, 0, columns]], axis=0
        )
        head_values = jnp.concatenate(
            [gathered[:, 1, columns], response_key_values[:, 1, columns]], axis=0
        )
        head_query = query_heads[:, key_value_head]
        head_grad = head_gradients[:, key_value_head]
        scores = jnp.where(visible[None], head_scores(head_query, head_keys), MASKED_SCORE)
        row_max = jnp.max(scores, axis=-1, keepdims=True)
        raised = jnp.exp(scores - row_max)
        weights = raised / jnp.sum(raised, axis=-1, keepdims=True)
        weights_low = weights.astype(jnp.bfloat16)
        attended = jnp.einsum(
            "grl,ld->rgd", weights_low, head_values, preferred_element_type=jnp.float32
        )
        row_delta = jnp.einsum("rgd,rgd->gr", head_grad.astype(jnp.float32), attended)[..., None]
        dscore_low = head_backward(weights, head_grad, head_values, row_delta)
        grad_query = jnp.einsum(
            "grl,ld->rgd", dscore_low, head_keys, preferred_element_type=jnp.float32
        )
        key_list.append(
            jnp.einsum(
                "grl,rgd->ld",
                dscore_low[..., prompt_len:],
                head_query,
                preferred_element_type=jnp.float32,
            )
            * inv_root
        )
        value_list.append(
            jnp.einsum(
                "grl,rgd->ld",
                weights_low[..., prompt_len:],
                head_grad,
                preferred_element_type=jnp.float32,
            )
        )
        attended_list.append(attended)
        query_list.append(grad_query * inv_root)
        score_list.append(dscore_low[..., :prompt_len])
        weight_list.append(weights_low[..., :prompt_len])
    attended = jnp.stack(attended_list, axis=1)
    grad_query = jnp.stack(query_list, axis=1)
    response_keys = jnp.concatenate(key_list, axis=1)
    own_values = jnp.concatenate(value_list, axis=1)
    score_store = jnp.stack(score_list, axis=0)
    weight_store = jnp.stack(weight_list, axis=0)
    key_term = (
        jnp.einsum("kgrl,rkgd->lkd", score_store, query_heads, preferred_element_type=jnp.float32)
        * inv_root
    )
    value_term = jnp.einsum(
        "kgrl,rkgd->lkd", weight_store, head_gradients, preferred_element_type=jnp.float32
    )
    prompt_grad = lax.psum_scatter(
        jnp.stack(
            [
                key_term.reshape(prompt_len, key_value_width),
                value_term.reshape(prompt_len, key_value_width),
            ],
            axis=1,
        ).astype(jnp.bfloat16),
        "resp",
        scatter_dimension=0,
        tiled=True,
    )
    attn_out = jnp.where(is_valid[:, None], attended.reshape(resp_len, -1), 0.0).astype(
        jnp.bfloat16
    )
    grad_queries = grad_query.reshape(resp_len, -1).astype(jnp.bfloat16)
    grad_resp_kv = jnp.stack([response_keys, own_values], axis=1).astype(jnp.bfloat16)
    return (attn_out, grad_queries, grad_resp_kv, prompt_grad)


def solution(mesh):
    in_specs = (
        P(("grp", "resp"), None, None),
        P(("grp", "resp"), None),
        P(("grp", "resp"), None, None),
        P(("grp", "resp"), None),
        P(("grp", "resp")),
    )
    out_specs = (
        P(("grp", "resp"), None),
        P(("grp", "resp"), None),
        P(("grp", "resp"), None, None),
        P(("grp", "resp"), None, None),
    )
    return jax.shard_map(
        per_device, mesh=mesh, in_specs=in_specs, out_specs=out_specs, check_vma=False
    )
```

profile of v0, /device:TPU:1, one launch (start us, length us, event | category | flops | bytes accessed | tf_op | source)
XLA Modules:
  0.0 344.5 jit_solution(8464850246347053854)
XLA Ops:
  7.2 1.7 copy.117
  9.0 2.2 copy.139
  11.8 1.4 copy.120
  15.7 38.9 %all-gather.2.cloned.1.call-done = bf16[2048,2,512]{2,0,1:T(8,128)(2,1)} async-done(((bf16[128,2,512]{2,0,1:T(8,128)(2,1)}), bf16[2048,2,512]{2,0,1:T(8,128)(2,1)}) %all-gather.2.cloned.1.call-update) | async-done | bytes 4194320 | tf_op jit(solution)/shard_map/all_gather | solution.py:41
  54.5 4.0 %slice_bitcast_fusion.15 = (bf16[2048,128]{1,0:T(8,128)(2,1)}, bf16[2048,128]{1,0:T(8,128)(2,1)S(1)}, bf16[2048,128]{1,0:T(8,128)(2,1)}, bf16[2048,128]{1,0:T(8,...) fusion(bf16[2048,2,512]{2,0,1:T(8,128)(2,1)} %all-gather.2.clon, ...), kind=kLoop, calls=%fused_computation.116 | loop fusion | bytes 8388608 | tf_op jit(solution)/shard_map/squeeze | solution.py:51
  58.5 4.4 %fusion.138 = (f32[5,128]{1,0:T(8,128)S(1)}, f32[5,128,2176]{1,2,0:T(8,128)}) fusion(pred[128,2176]{0,1:T(8,128)(4,1)S(1)} %concatenate.36, bf16[128,128]{1,0:T(8,128)(2,1)S(1)} %get-tuple-element.46, bf16[2048,128]{1,0:T(8,128)(2,1)S(1)} %get-tuple-element.17, bf16[128,4,5,128]{0,3,2,1:T(8,128)(2,1)S(1)} %bitcast.391), kind=kOutput, calls=%fused_computation.211 | convolution fusion | flops 363202688 | bytes 6572544 | tf_op jit(solution)/shard_map/sub | solution.py:57
  62.9 3.0 fusion.44
  65.9 1.7 slice_bitcast_fusion
  67.6 5.5 %fusion.139 = (f32[5,128]{1,0:T(8,128)S(1)}, f32[5,128,2176]{1,2,0:T(8,128)}) fusion(pred[128,2176]{0,1:T(8,128)(4,1)} %copy-done.33, bf16[128,128]{1,0:T(8,128)(2,1)S(1)} %get-tuple-element.48, bf16[2048,128]{1,0:T(8,128)(2,1)} %get-tuple-element.19, bf16[128,4,5,128]{0,3,2,1:T(8,128)(2,1)} %bitcast.392), kind=kOutput, calls=%fused_computation.212 | convolution fusion | flops 363202688 | bytes 6572544 | tf_op jit(solution)/shard_map/sub | solution.py:57
  73.1 3.0 fusion.43
  76.2 1.5 copy-done
  77.7 1.7 slice_bitcast_fusion.1
  79.4 5.6 %fusion.140 = (f32[5,128]{1,0:T(8,128)S(1)}, f32[5,128,2176]{1,2,0:T(8,128)}) fusion(pred[128,2176]{0,1:T(8,128)(4,1)} %copy-done.33, bf16[128,128]{1,0:T(8,128)(2,1)S(1)} %get-tuple-element.50, bf16[2048,128]{1,0:T(8,128)(2,1)} %get-tuple-element.21, bf16[128,4,5,128]{0,3,2,1:T(8,128)(2,1)} %bitcast.393), kind=kOutput, calls=%fused_computation.213 | convolution fusion | flops 363202688 | bytes 6572544 | tf_op jit(solution)/shard_map/sub | solution.py:57
  85.0 3.0 fusion.42
  88.1 1.6 copy-done.2
  89.7 1.6 slice_bitcast_fusion.2
  91.3 5.5 %fusion.141 = (f32[5,128]{1,0:T(8,128)S(1)}, f32[5,128,2176]{1,2,0:T(8,128)}) fusion(pred[128,2176]{0,1:T(8,128)(4,1)} %copy-done.33, bf16[128,128]{1,0:T(8,128)(2,1)S(1)} %get-tuple-element.52, bf16[2048,128]{1,0:T(8,128)(2,1)} %get-tuple-element.23, bf16[128,4,5,128]{0,3,2,1:T(8,128)(2,1)} %bitcast.394), kind=kOutput, calls=%fused_computation.214 | convolution fusion | flops 363202688 | bytes 6572544 | tf_op jit(solution)/shard_map/sub | solution.py:57
  96.9 3.0 fusion.41
  99.9 1.9 slice_bitcast_fusion.3
  102.5 1.3 copy-done.1
  109.3 1.7 copy.258
  111.0 1.7 bitcast_convert_fusion.1
  112.7 1.9 copy.212
  115.7 5.3 %fusion.25 = bf16[5,128,2176]{1,2,0:T(8,128)(2,1)} fusion(f32[5,128]{1,0:T(8,128)S(1)} %fusion.70, f32[5,128,2176]{1,2,0:T(8,128)} %get-tuple-element.39, f32[5,128]{1,0:T(8,128)S(1)} %get-tuple-element.38, bf16[128,128]{1,0:T(8,128)(2,1)} %copy-done.39, bf16[2048,128]{1,0:T(8,128)(2,1)} %get-tuple-element.18, bf16[128,4,5,128]{0,3,2,1:T(8,128)(2,1)} %bitcast.380), kind=kOutput, calls=%fused_computation.26 | convolution fusion | flops 363200512 | bytes 9081856 | tf_op jit(solution)/shard_map/rgd,ld->grl/dot_general | solution.py:24
  120.9 1.7 copy.257
  122.6 1.7 bitcast_convert_fusion.2
  124.3 1.9 copy.204
  127.3 5.3 %fusion.27 = bf16[5,128,2176]{1,2,0:T(8,128)(2,1)} fusion(f32[5,128]{1,0:T(8,128)S(1)} %fusion.71, f32[5,128,2176]{1,2,0:T(8,128)} %get-tuple-element.41, f32[5,128]{1,0:T(8,128)S(1)} %get-tuple-element.40, bf16[128,128]{1,0:T(8,128)(2,1)} %copy-done.38, bf16[2048,128]{1,0:T(8,128)(2,1)} %copy-done.23, bf16[128,4,5,128]{0,3,2,1:T(8,128)(2,1)} %bitcast.381), kind=kOutput, calls=%fused_computation.29 | convolution fusion | flops 363200512 | bytes 9081856 | tf_op jit(solution)/shard_map/rgd,ld->grl/dot_general | solution.py:24
  132.6 1.7 copy.256
  134.4 1.7 bitcast_convert_fusion.3
  136.1 1.9 copy.196
  139.0 5.4 %fusion.29 = bf16[5,128,2176]{1,2,0:T(8,128)(2,1)} fusion(f32[5,128]{1,0:T(8,128)S(1)} %fusion.72, f32[5,128,2176]{1,2,0:T(8,128)} %get-tuple-element.43, f32[5,128]{1,0:T(8,128)S(1)} %get-tuple-element.42, bf16[128,128]{1,0:T(8,128)(2,1)} %get-tuple-element.51, bf16[2048,128]{1,0:T(8,128)(2,1)} %get-tuple-element.22, bf16[128,4,5,128]{0,3,2,1:T(8,128)(2,1)} %bitcast.382), kind=kOutput, calls=%fused_computation.32 | convolution fusion | flops 363200512 | bytes 9081856 | tf_op jit(solution)/shard_map/rgd,ld->grl/dot_general | solution.py:24
  146.5 5.4 %fusion.31 = bf16[5,128,2176]{1,2,0:T(8,128)(2,1)} fusion(f32[5,128]{1,0:T(8,128)S(1)} %fusion.73, f32[5,128,2176]{1,2,0:T(8,128)} %get-tuple-element.45, f32[5,128]{1,0:T(8,128)S(1)} %get-tuple-element.44, bf16[128,128]{1,0:T(8,128)(2,1)} %get-tuple-element.53, bf16[2048,128]{1,0:T(8,128)(2,1)} %get-tuple-element.16, bf16[128,4,5,128]{0,3,2,1:T(8,128)(2,1)} %bitcast.383), kind=kOutput, calls=%fused_computation.35 | convolution fusion | flops 363200512 | bytes 9081856 | tf_op jit(solution)/shard_map/rgd,ld->grl/dot_general | solution.py:24
  152.1 1.3 copy-done.16
  153.5 4.8 %bitcast_convert_fusion = bf16[4,128,2048]{2,1,0:T(8,128)(2,1)} fusion(bf16[128,4,5,128]{0,3,2,1:T(8,128)(2,1)S(1)} %bitcast.388, bf16[1,5,128,2048]{2,3,1,0:T(8,128)(2,1)S(1)} %copy-done.13, bf16[1,5,128,2048]{2,3,1,0:T(8,128)(2,1)S(1)} %copy-done.14, bf16[1,5,128,2048]{2,3,1,0:T(8,128)(2,1)S(1)} %copy-done.15, bf16[1,5,128,2048]{2,3,1,0:T(8,128)(2,1)S(1)} %copy-done.16), kind=kOutput, calls=%fused_computation.45 | convolution fusion | flops 1358954496 | bytes 13238272 | tf_op jit(solution)/shard_map/kgrl,rkgd->lkd/dot_general | solution.py:99
  158.2 10.8 %copy.171 = bf16[2048,1,512]{2,1,0:T(2,128)(2,1)} copy(bf16[2048,1,512]{0,2,1:T(8,128)(2,1)} %bitcast.389) | data formatting | bytes 4194304 | tf_op jit(solution)/shard_map/stack;reshape | solution.py:103
  169.0 2.1 slice_bitcast_fusion.4
  171.8 1.6 copy-done.7
  173.6 1.6 copy-done.9
  176.3 4.9 %fusion.36 = bf16[4,2048,128]{1,2,0:T(8,128)(2,1)} fusion(bf16[128,4,5,128]{0,3,2,1:T(8,128)(2,1)S(1)} %bitcast.397, bf16[1,5,128,2048]{2,3,1,0:T(8,128)(2,1)S(1)} %slice_bitcast_fusion.4, bf16[1,5,128,2048]{2,3,1,0:T(8,128)(2,1)S(1)} %slice_bitcast_fusion.5, bf16[1,5,128,2048]{2,3,1,0:T(8,128)(2,1)S(1)} %slice_bitcast_fusion.6, ...), kind=kOutput, calls=%fused_computation.47 | convolution fusion | flops 1360003072 | bytes 13238272 | tf_op jit(solution)/shard_map/kgrl,rkgd->lkd/dot_general | solution.py:96
  181.1 10.7 %copy.170 = bf16[2048,1,512]{2,1,0:T(2,128)(2,1)} copy(bf16[2048,1,512]{0,2,1:T(8,128)(2,1)} %bitcast.390) | data formatting | bytes 4194304 | tf_op jit(solution)/shard_map/stack;reshape | solution.py:103
  191.9 10.8 %pad_maximum_fusion = bf16[2048,2,512]{2,1,0:T(2,128)(2,1)} fusion(bf16[2048,1,512]{2,1,0:T(2,128)(2,1)} %copy.171, bf16[2048,1,512]{2,1,0:T(2,128)(2,1)} %copy.170), kind=kLoop, calls=%fused_computation.44 | loop fusion | flops 8388608 | bytes 8388608 | tf_op jit(solution)/shard_map/stack | solution.py:103
  205.7 2.7 fusion.50
  208.5 1.8 fusion.51
  214.1 1.2 fusion.60
  217.8 1.2 fusion.62
  223.4 112.4 %all-reduce.4.cloned.1.call-done = bf16[2048,2,512]{2,1,0:T(2,128)(2,1)} async-done(((bf16[2048,2,512]{2,1,0:T(2,128)(2,1)}), bf16[2048,2,512]{2,1,0:T(2,128)(2,1)}) %all-reduce.4.cloned.1.call-update) | async-done | bytes 4194320
  335.8 1.8 constant_dynamic-slice_fusion
  (123 shorter events, 28.9 us)
Async XLA Ops:
  7.2 6.8 %copy-start.28 = (bf16[128,2,512]{2,1,0:T(2,128)(2,1)S(1)}, bf16[128,2,512]{2,1,0:T(2,128)(2,1)}, u32[]{:S(2)}) copy-start(bf16[128,2,512]{2,1,0:T(2,128)(2,1)} %param.7) | copy-start | bytes 786436
  7.2 47.4 %all-gather.2.cloned.1.call-start = ((), (), s32[]{:S(2)}) async-start(), calls=%async_computation | async-start | bytes 4456448 | tf_op jit(solution)/shard_map/all_gather | solution.py:41
  9.0 326.9 %all-reduce.4.cloned.1.call-start = ((), (), s32[]{:S(2)}) async-start(), calls=%async_computation.1 | async-start | bytes 8388608
  13.2 45.3 %copy-start.30 = (bf16[128,2560]{0,1:T(8,128)(2,1)}, bf16[128,2560]{0,1:T(8,128)(2,1)S(1)}, u32[]{:S(2)}) copy-start(bf16[128,2560]{0,1:T(8,128)(2,1)S(1)} %copy.120) | copy-start | bytes 1966084
  13.4 45.2 %copy-start.33 = (pred[128,2176]{0,1:T(8,128)(4,1)}, pred[128,2176]{0,1:T(8,128)(4,1)S(1)}, u32[]{:S(2)}) copy-start(pred[128,2176]{0,1:T(8,128)(4,1)S(1)} %concatenate.36) | copy-start | bytes 835588
  14.4 87.4 %copy-start.39 = (bf16[128,128]{1,0:T(8,128)(2,1)}, bf16[128,128]{1,0:T(8,128)(2,1)S(1)}, u32[]{:S(2)}) copy-start(bf16[128,128]{1,0:T(8,128)(2,1)S(1)} %get-tuple-element.47) | copy-start | bytes 98308
  14.4 88.1 %copy-start.38 = (bf16[128,128]{1,0:T(8,128)(2,1)}, bf16[128,128]{1,0:T(8,128)(2,1)S(1)}, u32[]{:S(2)}) copy-start(bf16[128,128]{1,0:T(8,128)(2,1)S(1)} %get-tuple-element.49) | copy-start | bytes 98308
  15.7 75.7 %copy-start.34 = (bf16[128,128]{1,0:T(8,128)(2,1)}, bf16[128,128]{1,0:T(8,128)(2,1)S(1)}, u32[]{:S(2)}) copy-start(bf16[128,128]{1,0:T(8,128)(2,1)S(1)} %get-tuple-element.52) | copy-start | bytes 98308
  58.5 4.4 %copy-start.27 = (bf16[2048,128]{1,0:T(8,128)(2,1)}, bf16[2048,128]{1,0:T(8,128)(2,1)S(1)}, u32[]{:S(2)}) copy-start(bf16[2048,128]{1,0:T(8,128)(2,1)S(1)} %get-tuple-element.17) | copy-start | bytes 1572868
  58.5 44.0 %copy-start.23 = (bf16[2048,128]{1,0:T(8,128)(2,1)}, bf16[2048,128]{1,0:T(8,128)(2,1)S(1)}, u32[]{:S(2)}) copy-start(bf16[2048,128]{1,0:T(8,128)(2,1)S(1)} %get-tuple-element.20) | copy-start | bytes 1572868
  76.2 1.5 copy-start
  88.1 1.6 copy-start.2
  99.9 5.5 %copy-start.4 = (bf16[5,128,2176]{1,2,0:T(8,128)(2,1)}, bf16[5,128,2176]{1,2,0:T(8,128)(2,1)S(1)}, u32[]{:S(2)}) copy-start(bf16[5,128,2176]{1,2,0:T(8,128)(2,1)S(1)} %fusion.41) | copy-start | bytes 8355844
  99.9 1.9 copy-start.24
  101.8 2.0 copy-start.1
  101.8 2.8 copy-start.3
  101.8 2.9 copy-start.22
  101.8 2.9 copy-start.37
  102.5 3.6 %copy-start.12 = (f32[128,5,128]{2,0,1:T(8,128)}, f32[128,5,128]{2,0,1:T(8,128)S(1)}, u32[]{:S(2)}) copy-start(f32[128,5,128]{2,0,1:T(8,128)S(1)} %fusion.66) | copy-start | bytes 983044
  103.8 1.6 copy-start.21
  103.8 1.6 copy-start.36
  104.4 1.6 copy-start.11
  105.4 1.1 copy-start.20
  105.4 1.1 copy-start.40
  107.6 0.8 copy-start.17
  138.9 5.4 %copy-start.29 = (bf16[128,1,5,128]{0,3,2,1:T(8,128)(2,1)S(1)}, bf16[128,1,5,128]{0,3,2,1:T(8,128)(2,1)}, u32[]{:S(2)}) copy-start(bf16[128,1,5,128]{0,3,2,1:T(8,128)(2,1)} %get-tuple-element.24) | copy-start | bytes 491524
  146.5 5.5 %copy-start.13 = (bf16[1,5,128,2048]{2,3,1,0:T(8,128)(2,1)S(1)}, bf16[1,5,128,2048]{2,3,1,0:T(8,128)(2,1)}, u32[]{:S(2)}) copy-start(bf16[1,5,128,2048]{2,3,1,0:T(8,128)(2,1)} %slice_bitcast_fusion) | copy-start | bytes 7864324
  146.5 5.5 %copy-start.14 = (bf16[1,5,128,2048]{2,3,1,0:T(8,128)(2,1)S(1)}, bf16[1,5,128,2048]{2,3,1,0:T(8,128)(2,1)}, u32[]{:S(2)}) copy-start(bf16[1,5,128,2048]{2,3,1,0:T(8,128)(2,1)} %slice_bitcast_fusion.1) | copy-start | bytes 7864324
  146.5 5.6 %copy-start.15 = (bf16[1,5,128,2048]{2,3,1,0:T(8,128)(2,1)S(1)}, bf16[1,5,128,2048]{2,3,1,0:T(8,128)(2,1)}, u32[]{:S(2)}) copy-start(bf16[1,5,128,2048]{2,3,1,0:T(8,128)(2,1)} %slice_bitcast_fusion.2) | copy-start | bytes 7864324
  146.5 6.9 %copy-start.16 = (bf16[1,5,128,2048]{2,3,1,0:T(8,128)(2,1)S(1)}, bf16[1,5,128,2048]{2,3,1,0:T(8,128)(2,1)}, u32[]{:S(2)}) copy-start(bf16[1,5,128,2048]{2,3,1,0:T(8,128)(2,1)} %slice_bitcast_fusion.3) | copy-start | bytes 7864324
  146.5 6.9 %copy-start.18 = (bf16[128,2560]{0,1:T(8,128)(2,1)S(1)}, bf16[128,2560]{0,1:T(8,128)(2,1)}, u32[]{:S(2)}) copy-start(bf16[128,2560]{0,1:T(8,128)(2,1)} %copy-done.17) | copy-start | bytes 1966084
  169.0 2.6 copy-start.5
  171.6 1.8 copy-start.7
  173.4 1.8 copy-start.9
  175.2 1.1 copy-start.31
  202.7 0.7 copy-start.41
  202.7 1.9 copy-start.19
  205.7 2.8 copy-start.6
  205.7 4.6 %copy-start.8 = (bf16[5,128,2176]{1,2,0:T(8,128)(2,1)S(1)}, bf16[5,128,2176]{1,2,0:T(8,128)(2,1)}, u32[]{:S(2)}) copy-start(bf16[5,128,2176]{1,2,0:T(8,128)(2,1)} %fusion.29) | copy-start | bytes 8355844
  205.7 4.7 %copy-start.26 = (bf16[2048,128]{1,0:T(8,128)(2,1)S(1)}, bf16[2048,128]{1,0:T(8,128)(2,1)}, u32[]{:S(2)}) copy-start(bf16[2048,128]{1,0:T(8,128)(2,1)} %get-tuple-element.21) | copy-start | bytes 1572868
  208.5 2.5 copy-start.10
  208.5 2.6 copy-start.25
  208.5 2.6 copy-start.35
  212.9 7.3 %copy-start.32 = (bf16[128,2560]{0,1:T(8,128)(2,1)S(1)}, bf16[128,2560]{0,1:T(8,128)(2,1)}, u32[]{:S(2)}) copy-start(bf16[128,2560]{0,1:T(8,128)(2,1)} %copy-done.30) | copy-start | bytes 1966084
Sparse Core Ops, SparseCore 0:
  10.4 44.1 all-gather.1
  202.9 132.9 all-reduce.3
where the time goes:
time: 346 us; the launch traced here: 345 us
  waiting for transfers between devices  151 us (44%)
  local copies, waits for them, and re-layouts  73 us (21%)
  matrix products  70.1 us (20%)
  other arithmetic  34.1 us (10%)
  between operations  15.9 us (5%)
    unnamed x3, waiting for transfers between devices  112 us
    all_gather x1, waiting for transfers between devices, per_device(): gathered = lax.all_gather(prompt_kv, 'resp', axis=0, tiled=True)  38.9 us
    unnamed x100, local copies, waits for them, and re-layouts  35.5 us
    another operation x2, local copies, waits for them, and re-layouts, per_device(): jnp.stack([key_term.reshape(prompt_len, key_value_width), value_term.resh...  21.5 us
    dot_general x4, matrix products, head_backward(): jnp.einsum('rgd,ld->grl', head_grad, head_values, preferred_element_type=...  21.4 us
    sub x4, matrix products, per_device(): raised = jnp.exp(scores - row_max)  21.1 us
    convert_element_type x4, other arithmetic, per_device(): weights_low = weights.astype(jnp.bfloat16)  12.1 us
    another operation x1, other arithmetic, per_device(): jnp.stack([key_term.reshape(prompt_len, key_value_width), value_term.resh...  10.8 us
  transfers between devices with their start and end apart: 2, of which 2 were waited for; matrix products, arithmetic and copies ran while one was open for 7% of the time, Pallas kernels for 0%

commit v1 on v0

v1 whole, which is shorter than its diff:
```python
import functools
import math

import jax
import jax.numpy as jnp
from jax import lax
from jax.experimental import pallas as pl
from jax.experimental.pallas import tpu as pltpu
from jax.sharding import PartitionSpec as P

D = 128
T = 128
G = 5
KVH = 4
BLK = 2 * T
COLS = G * T
R = 2 * COLS
NP = 8
MASKED = -1e30
INV_ROOT = 1.0 / math.sqrt(D)
SCALE2 = INV_ROOT * math.log2(math.e)
BF = jnp.bfloat16
F32 = jnp.float32
MESH = pl.DeviceIdType.MESH


def dot(a, b, ca, cb):
    return lax.dot_general(a, b, (((ca,), (cb,)), ((), ())), preferred_element_type=F32)


def kernel(pkv, pack, oout, qout, rout, pout,
           kvb, xb, sb, srb, eb, erb, mb, lb, ot, gp, dlt, dqt, osend, qsend, rsend, pb, rb, fsend,
           st_s, st_r, loc, ag_s, ag_r, rs_s, rs_r, out_s, out_r):
    me = lax.axis_index("resp")
    z, x, c = me // 8, (me // 2) % 4, me % 2
    XP = z * 8 + ((x + 1) % 4) * 2 + c
    XM = z * 8 + ((x + 3) % 4) * 2 + c
    ZP = (1 - z) * 8 + x * 2 + c
    SIB = z * 8 + x * 2 + (1 - c)

    def remote(src, dst, ss, rs, to):
        return pltpu.make_async_remote_copy(
            src_ref=src, dst_ref=dst, send_sem=ss, recv_sem=rs, device_id={"resp": to}, device_id_type=MESH)

    barrier = pltpu.get_barrier_semaphore()
    for to in (XP, XM, ZP, SIB):
        pl.semaphore_signal(barrier, inc=1, device_id={"resp": to}, device_id_type=MESH)
    pl.semaphore_wait(barrier, 4)

    mine, other = 2 * c, 2 * (1 - c)
    rows = pl.ds(pl.multiple_of(c * T, T), T)
    orows = pl.ds(pl.multiple_of((1 - c) * T, T), T)
    ex_kv = remote(pkv.at[pl.ds(other, 2)], kvb.at[:, 0, :, rows, :], st_s.at[0], st_r.at[0], SIB)
    ex_kv.start()
    own_kv = pltpu.make_async_copy(pkv.at[pl.ds(mine, 2)], kvb.at[:, 0, :, rows, :], loc.at[0])
    own_kv.start()
    ex_x = remote(pack.at[pl.ds(other, 2)], xb.at[:, 1], st_s.at[1], st_r.at[1], SIB)
    ex_x.start()
    own_x = pltpu.make_async_copy(pack.at[pl.ds(mine, 2)], xb.at[:, 0], loc.at[1])
    own_x.start()

    def ag(a, kv, kind):
        to = (XP, XM, ZP, XP, XM, XP, XM, ZP)[kind]
        src = (0, 0, 0, 3, 3, 1, 2, 6)[kind]
        dst = (1, 2, 3, 4, 5, 6, 6, 7)[kind]
        part = {5: pl.ds(0, T), 6: pl.ds(T, T)}.get(kind, pl.ds(0, BLK))
        return remote(kvb.at[a, src, kv, part, :], kvb.at[a, dst, kv, part, :],
                      ag_s.at[a, kv, kind], ag_r.at[a, kv, kind], to)

    def ag_first(a, kv):
        for k in (0, 1, 2):
            ag(a, kv, k).start()

    def ag_second(a, kv):
        ag(a, kv, 0).wait_recv()
        ag(a, kv, 5).start()
        ag(a, kv, 1).wait_recv()
        ag(a, kv, 6).start()
        ag(a, kv, 2).wait_recv()
        ag(a, kv, 3).start()
        ag(a, kv, 4).start()

    def ag_third(a, kv):
        ag(a, kv, 5).wait_recv()
        ag(a, kv, 6).wait_recv()
        ag(a, kv, 7).start()

    def ag_wait(a, kv, *kinds):
        for k in kinds:
            ag(a, kv, k).wait_recv()

    def rs(a, kind):
        to = (XM, XP, ZP, XM, XP, XM, XP, ZP)[kind]
        src = (1, 2, 3, 4, 5, 6, 6, 7)[kind]
        part = {5: pl.ds(0, T), 6: pl.ds(T, T)}.get(kind, pl.ds(0, BLK))
        return remote(pb.at[a, src, :, part, :], rb.at[a, kind, :, part, :],
                      rs_s.at[a, kind], rs_r.at[a, kind], to)

    def rs_six(a):
        rs(a, 7).wait_recv()
        pb[a, 6] = (pb[a, 6].astype(F32) + rb[a, 7].astype(F32)).astype(BF)
        rs(a, 5).start()
        rs(a, 6).start()

    def rs_three(a):
        rs(a, 3).wait_recv()
        rs(a, 4).wait_recv()
        pb[a, 3] = (pb[a, 3].astype(F32) + rb[a, 3].astype(F32) + rb[a, 4].astype(F32)).astype(BF)
        rs(a, 2).start()

    def rs_one_two(a):
        rs(a, 5).wait_recv()
        pb[a, 1, :, :T] = (pb[a, 1, :, :T].astype(F32) + rb[a, 5, :, :T].astype(F32)).astype(BF)
        rs(a, 0).start()
        rs(a, 6).wait_recv()
        pb[a, 2, :, T:] = (pb[a, 2, :, T:].astype(F32) + rb[a, 6, :, T:].astype(F32)).astype(BF)
        rs(a, 1).start()

    def p_copy(a):
        return remote(fsend.at[a], pout.at[2 * c + a], out_s.at[a, 3], out_r.at[a, 3], SIB)

    def rs_final(a):
        for k in (0, 1, 2):
            rs(a, k).wait_recv()

        def total(part):
            return (pb[a, 0, :, part, :].astype(F32) + rb[a, 0, :, part, :].astype(F32)
                    + rb[a, 1, :, part, :].astype(F32) + rb[a, 2, :, part, :].astype(F32)).astype(BF)

        fsend[a] = total(orows)
        p_copy(a).start()
        pout[2 * c + a] = total(rows)

    def o_copy(a):
        return remote(osend.at[a], oout.at[pl.ds((2 * c + a) * G, G)], out_s.at[a, 0], out_r.at[a, 0], SIB)

    def q_copy(a):
        return remote(qsend.at[a], qout.at[pl.ds((2 * c + a) * G, G)], out_s.at[a, 1], out_r.at[a, 1], SIB)

    def r_copy(a):
        return remote(rsend.at[a], rout.at[2 * c + a], out_s.at[a, 2], out_r.at[a, 2], SIB)

    def at_step(i, hooks):
        for k, calls in hooks.items():
            @pl.when(i == k)
            def _():
                for call in calls:
                    call()

    def queries_of(a):
        return jnp.concatenate([xb[a, b, 0:G].reshape(COLS, D) for b in (0, 1)], axis=0)

    def fold(value, op):
        n = value.shape[0]
        return op(value.reshape(n // 8, 8, R), axis=0)

    def head(a, hooks_a, hooks_b, hooks_c, ends_c):
        slot = lax.broadcasted_iota(jnp.int32, (T, G, T), 2).reshape(T, COLS)
        key = lax.broadcasted_iota(jnp.int32, (T, COLS), 0)
        for b in (0, 1):
            s = dot(xb[a, b, 2 * G], xb[a, b, 0:G].reshape(COLS, D), 1, 1)
            srb[:, b * COLS:(b + 1) * COLS] = jnp.where(key <= slot, s, MASKED)
        mb[...] = fold(srb[...], jnp.max)

        def score_step(p, _):
            at_step(p, hooks_a)
            s = dot(kvb[a, p, 0], queries_of(a), 1, 1)
            sb[p] = s
            mb[...] = jnp.maximum(mb[...], fold(s, jnp.max))
            return 0

        lax.fori_loop(0, NP, score_step, 0)

        top = jnp.max(mb[...], axis=0, keepdims=True) * SCALE2
        mb[0:1] = top
        er = jnp.exp2(srb[...] * SCALE2 - top)
        lb[...] = fold(er, jnp.sum)
        erb[...] = er.astype(BF)
        for b in (0, 1):
            cols = slice(b * COLS, (b + 1) * COLS)
            ot[:, cols] = dot(xb[a, b, 2 * G + 1], erb[:, cols], 0, 0)

        def weight_step(p, _):
            at_step(p, hooks_b)
            e = jnp.exp2(sb[p] * SCALE2 - mb[0:1])
            lb[...] += fold(e, jnp.sum)
            low = e.astype(BF)
            eb[p] = low
            ot[...] += dot(kvb[a, p, 1], low, 0, 0)
            return 0

        lax.fori_loop(0, NP, weight_step, 0)

        inv = 1.0 / jnp.sum(lb[...], axis=0, keepdims=True)
        for b in (0, 1):
            for g in range(G):
                lo = b * COLS + g * T
                cols = slice(lo, lo + T)
                att = ot[:, cols] * inv[:, cols]
                gt = xb[a, b, G + g].astype(F32).T
                dlt[:, cols] = jnp.sum(gt * att, axis=0, keepdims=True) * inv[:, cols]
                gp[cols, :] = (gt * inv[:, cols]).T.astype(BF)
                if b == 0:
                    oout[(2 * c + a) * G + g] = att.T.astype(BF)
                else:
                    osend[a, g] = att.T.astype(BF)
        o_copy(a).start()

        for b in (0, 1):
            cols = slice(b * COLS, (b + 1) * COLS)
            dp = dot(xb[a, b, 2 * G + 1], gp[cols, :], 1, 1) - dlt[:, cols]
            ds = (erb[:, cols].astype(F32) * dp).astype(BF)
            dv = dot(erb[:, cols], gp[cols, :], 1, 0).astype(BF)
            dk = (dot(ds, xb[a, b, 0:G].reshape(COLS, D), 1, 0) * INV_ROOT).astype(BF)
            dqt[:, cols] = dot(xb[a, b, 2 * G], ds, 0, 0)
            if b == 0:
                rout[2 * c + a, 0] = dk
                rout[2 * c + a, 1] = dv
            else:
                rsend[a, 0] = dk
                rsend[a, 1] = dv
        r_copy(a).start()

        def grad_step(i, _):
            at_step(i, hooks_c)
            p = NP - 1 - i
            dp = dot(kvb[a, p, 1], gp[...], 1, 1) - dlt[...]
            ds = (eb[p].astype(F32) * dp).astype(BF)
            pb[a, p, 1] = dot(eb[p], gp[...], 1, 0).astype(BF)
            pb[a, p, 0] = (dot(ds, queries_of(a), 1, 0) * INV_ROOT).astype(BF)
            dqt[...] += dot(kvb[a, p, 0], ds, 0, 0)
            at_step(i, ends_c)
            return 0

        lax.fori_loop(0, NP, grad_step, 0)
        for b in (0, 1):
            for g in range(G):
                lo = b * COLS + g * T
                grad = (dqt[:, lo:lo + T] * INV_ROOT).T.astype(BF)
                if b == 0:
                    qout[(2 * c + a) * G + g] = grad
                else:
                    qsend[a, g] = grad
        q_copy(a).start()

    f = functools.partial
    ex_kv.wait_recv()
    own_kv.wait()
    ag_first(0, 0)
    ag_first(0, 1)
    ex_x.wait_recv()
    own_x.wait()

    ends_c = lambda a: {0: [rs(a, 7).start], 2: [rs(a, 4).start], 3: [rs(a, 3).start, f(rs_six, a)]}
    head(0,
         {1: [f(ag_second, 0, 0), f(ag_first, 1, 0)],
          4: [f(ag_third, 0, 0), f(ag_second, 0, 1), f(ag_first, 1, 1), f(ag_wait, 0, 0, 3, 4)],
          7: [f(ag_wait, 0, 0, 7)]},
         {0: [f(ag_third, 0, 1), f(ag_second, 1, 0)],
          4: [f(ag_wait, 0, 1, 3, 4)],
          7: [f(ag_third, 1, 0), f(ag_second, 1, 1), f(ag_wait, 0, 1, 7)]},
         {2: [f(ag_third, 1, 1)]},
         ends_c(0))
    head(1,
         {0: [f(ag_wait, 1, 0, 3, 4)],
          2: [f(rs_three, 0), f(rs_one_two, 0)],
          7: [f(ag_wait, 1, 0, 7)]},
         {0: [f(ag_wait, 1, 1, 3, 4)],
          7: [f(ag_wait, 1, 1, 7)]},
         {0: [f(rs_final, 0)]},
         ends_c(1))
    rs_three(1)
    rs_one_two(1)
    rs_final(1)

    ex_kv.wait_send()
    ex_x.wait_send()
    for a in (0, 1):
        for kind in range(8):
            ag(a, 0, kind).wait_send()
            ag(a, 1, kind).wait_send()
            rs(a, kind).wait_send()
        for copy in (o_copy(a), q_copy(a), r_copy(a), p_copy(a)):
            copy.wait()


def per_device(prompt_kv, queries, response_key_values, grad_out, lengths):
    live = (jnp.arange(T, dtype=jnp.int32) < lengths[0])[:, None]
    grads = jnp.where(live, grad_out, jnp.zeros_like(grad_out))
    pkv = prompt_kv.reshape(T, 2, KVH, D).transpose(2, 1, 0, 3)
    rkv = response_key_values.reshape(T, 2, KVH, D).transpose(2, 1, 0, 3)
    by_head = lambda v: v.reshape(T, KVH, G, D).transpose(1, 2, 0, 3)
    pack = jnp.concatenate([by_head(queries), by_head(grads), rkv], axis=1)
    vmem = pl.BlockSpec(memory_space=pltpu.VMEM)
    dma = pltpu.SemaphoreType.DMA
    flops = 6 * 2 * 2 * R * (NP * BLK + T) * D
    oout, qout, rout, pout = pl.pallas_call(
        kernel,
        out_shape=(
            jax.ShapeDtypeStruct((KVH * G, T, D), BF),
            jax.ShapeDtypeStruct((KVH * G, T, D), BF),
            jax.ShapeDtypeStruct((KVH, 2, T, D), BF),
            jax.ShapeDtypeStruct((KVH, 2, T, D), BF),
        ),
        in_specs=[vmem, vmem],
        out_specs=(vmem,) * 4,
        scratch_shapes=[
            pltpu.VMEM((2, NP, 2, BLK, D), BF),
            pltpu.VMEM((2, 2, 2 * G + 2, T, D), BF),
            pltpu.VMEM((NP, BLK, R), F32),
            pltpu.VMEM((T, R), F32),
            pltpu.VMEM((NP, BLK, R), BF),
            pltpu.VMEM((T, R), BF),
            pltpu.VMEM((8, R), F32),
            pltpu.VMEM((8, R), F32),
            pltpu.VMEM((D, R), F32),
            pltpu.VMEM((R, D), BF),
            pltpu.VMEM((1, R), F32),
            pltpu.VMEM((D, R), F32),
            pltpu.VMEM((2, G, T, D), BF),
            pltpu.VMEM((2, G, T, D), BF),
            pltpu.VMEM((2, 2, T, D), BF),
            pltpu.VMEM((2, NP, 2, BLK, D), BF),
            pltpu.VMEM((2, NP, 2, BLK, D), BF),
            pltpu.VMEM((2, 2, T, D), BF),
            dma((2,)), dma((2,)), dma((2,)),
            dma((2, 2, 8)), dma((2, 2, 8)),
            dma((2, 8)), dma((2, 8)),
            dma((2, 4)), dma((2, 4)),
        ],
        compiler_params=pltpu.CompilerParams(
            collective_id=0, has_side_effects=True, vmem_limit_bytes=56 << 20),
        cost_estimate=pl.CostEstimate(flops=flops, bytes_accessed=8 << 20, transcendentals=2 * R * (NP * BLK + T)),
        name="shared_prompt_attention",
    )(pkv, pack)
    flat = lambda v: v.transpose(1, 0, 2).reshape(T, KVH * G * D)
    attn_out = jnp.where(live, flat(oout), jnp.zeros((), BF))
    rows = lambda v: v.transpose(2, 1, 0, 3).reshape(T, 2, KVH * D)
    return attn_out, flat(qout), rows(rout), rows(pout)


def solution(mesh):
    wide, thick = P(("grp", "resp"), None), P(("grp", "resp"), None, None)
    return jax.shard_map(
        per_device,
        mesh=mesh,
        in_specs=(thick, wide, thick, wide, P(("grp", "resp"))),
        out_specs=(wide, wide, thick, thick),
        check_vma=False,
    )
```

time: 346 us -> 71.1 us (0.21)
  waiting for transfers between devices: 151 us -> 0 us
  matrix products: 70.1 us -> 0 us
  local copies, waits for them, and re-layouts: 73 us -> 10.9 us
  Pallas kernels: 0 us -> 56.5 us
  other arithmetic: 34.1 us -> 1.49 us
  between operations: 15.9 us -> 1.47 us
    unnamed x3 -> x0, waiting for transfers between devices: 112 us -> none
    pallas_call x0 -> x1, Pallas kernels: none -> 56.5 us  [per_device(): pl.pallas_call(kernel, out_shape=(jax.ShapeDtypeStruct((KVH * G, T, D), B...]
    dot_general x22 -> x0, matrix products: 49 us -> none  [the longest x4 21.4 us: head_backward(): jnp.einsum('rgd,ld->grl', head_grad, head_values, preferred_element_type=...]
    all_gather x1 -> x0, waiting for transfers between devices: 38.9 us -> none  [per_device(): gathered = lax.all_gather(prompt_kv, 'resp', axis=0, tiled=True)]
    another operation x10 -> x0, local copies, waits for them, and re-layouts: 31 us -> none  [the longest x2 21.5 us: per_device(): jnp.stack([key_term.reshape(prompt_len, key_value_width), value_term.resh...]
    unnamed x100 -> x18, local copies, waits for them, and re-layouts: 35.5 us -> 7.13 us
    sub x4 -> x0, matrix products: 21.1 us -> none  [per_device(): raised = jnp.exp(scores - row_max)]
    convert_element_type x4 -> x0, other arithmetic: 12.1 us -> none  [per_device(): weights_low = weights.astype(jnp.bfloat16)]
  transfers between devices with their start and end apart: 2 -> 0, of which waited for: 2 -> 0; matrix products, arithmetic and copies ran while one was open for 7% -> 0% of each run, Pallas kernels for 0% -> 0%
where the time goes in v1:
time: 71.1 us; the launch traced here: 70.4 us
  Pallas kernels  56.5 us (79%)
  local copies, waits for them, and re-layouts  10.9 us (15%)
  other arithmetic  1.49 us (2%)
  between operations  1.47 us (2%)
    pallas_call x1, Pallas kernels, per_device(): pl.pallas_call(kernel, out_shape=(jax.ShapeDtypeStruct((KVH * G, T, D), B...  56.5 us
    unnamed x18, local copies, waits for them, and re-layouts  7.13 us
    transpose x2, local copies, waits for them, and re-layouts, per_device(): flat = lambda v: v.transpose(1, 0, 2).reshape(T, KVH * G * D)  1.74 us

profile of v1, /device:TPU:1, one launch (start us, length us, event | category | flops | bytes accessed | tf_op | source)
XLA Modules:
  0.0 70.4 jit_solution(5342474372439007794)
XLA Ops:
  0.6 0.0 copy-start
  1.4 1.2 %copy.9 = bf16[128,2,512]{0,2,1:T(8,128)(2,1)S(1)} copy(bf16[128,2,512]{2,1,0:T(2,128)(2,1)} %param.5) | data formatting | bytes 524288 | tf_op args[0]
  2.5 0.9 %copy.10 = bf16[128,2,4,128]{3,0,1,2:T(8,128)(2,1)} copy(bf16[128,2,4,128]{0,3,2,1:T(8,128)(2,1)S(1)} %bitcast.27) | data formatting | bytes 524288 | tf_op jit(solution)/shard_map/reshape | solution.py:290
  3.4 1.1 %copy.15 = bf16[128,2,512]{0,2,1:T(8,128)(2,1)S(1)} copy(bf16[128,2,512]{2,1,0:T(2,128)(2,1)} %param.7) | data formatting | bytes 524288 | tf_op args[2]
  4.5 0.0 copy-start.1
  4.5 0.2 copy.16
  4.7 0.0 copy-done
  4.7 0.3 copy.11
  5.1 0.3 copy.12
  5.4 0.2 copy-done.1
  5.6 0.3 copy.13
  6.0 0.3 copy.14
  6.3 1.3 %pad_maximum_fusion.pack = bf16[4,12,128,128]{3,2,1,0:T(8,128)(2,1)} fusion(bf16[4,2,128,128]{3,2,1,0:T(8,128)(2,1)S(1)} %bitcast.24, bf16[4,5,128,128]{3,2,1,0:T(8,128)(2,1)S(1)} %bitcast.23, bf16[4,5,128,128]{3,2,1,0:T(8,128)(2,1)S(1)} %bitcast.22), kind=kLoop, calls=%fused_computation | loop fusion | flops 1572864 | bytes 3145728 | tf_op jit(solution)/shard_map/concatenate | solution.py:293
  7.7 56.5 %shared_prompt_attention.1 = (bf16[20,128,128]{2,1,0:T(8,128)(2,1)}, bf16[20,128,128]{2,1,0:T(8,128)(2,1)}, bf16[4,2,128,128]{3,2,1,0:T(8,128)(2,1)}, bf16[4,2,128,128]{3,2,1,0:T(8,128)(2,1)}) custom-call(bf16[4,2,128,128]{3,2,1,0:T(8,128)(2,1)} %bitcast.31, bf16[4,12,128,128]{3,2,1,0:T(8,128)(2,1)} %pad_maximum_fusion.pack), custom_call_target="tpu_custom_call" | custom-call | flops 8556380160 | bytes 8388608 | tf_op jit(solution)/shard_map/shared_prompt_attention/pallas_call | solution.py:297
  64.2 1.4 %copy.17 = bf16[128,20,128]{0,2,1:T(8,128)(2,1)S(1)} copy(bf16[128,20,128]{2,0,1:T(8,128)(2,1)} %bitcast.30) | data formatting | bytes 1310720 | tf_op jit(solution)/shard_map/transpose | solution.py:336
  65.6 0.0 copy-start.2
  65.6 0.1 bitcast_select_fusion
  65.7 1.1 %copy.21 = bf16[128,2560]{1,0:T(8,128)(2,1)} copy(bf16[128,2560]{0,1:T(8,128)(2,1)S(1)} %bitcast_select_fusion) | data formatting | bytes 1310720
  66.8 0.0 copy-start.4
  66.8 0.0 copy-done.2
  66.8 0.0 copy-start.3
  66.8 0.3 copy.18
  67.1 1.1 %copy.22 = bf16[128,2560]{1,0:T(8,128)(2,1)} copy(bf16[128,2560]{0,1:T(8,128)(2,1)S(1)} %bitcast.20) | data formatting | bytes 1310720
  68.2 0.0 copy-done.4
  68.2 0.2 copy.19
  68.4 0.9 %copy.23 = bf16[128,2,512]{2,1,0:T(2,128)(2,1)} copy(bf16[128,2,512]{0,2,1:T(8,128)(2,1)S(1)} %bitcast.25) | data formatting | bytes 524288
  69.3 0.0 copy-done.3
  69.3 0.2 copy.20
  69.5 0.9 %copy.24 = bf16[128,2,512]{2,1,0:T(2,128)(2,1)} copy(bf16[128,2,512]{0,2,1:T(8,128)(2,1)S(1)} %bitcast.26) | data formatting | bytes 524288
  (2 shorter events, 0.1 us)
Async XLA Ops:
  0.6 4.1 %copy-start = (bf16[128,2560]{1,0:T(8,128)(2,1)S(1)}, bf16[128,2560]{1,0:T(8,128)(2,1)}, u32[]{:S(2)}) copy-start(bf16[128,2560]{1,0:T(8,128)(2,1)} %param.6) | copy-start | bytes 1966084
  4.5 1.1 %copy-start.1 = (bf16[128,2560]{1,0:T(8,128)(2,1)S(1)}, bf16[128,2560]{1,0:T(8,128)(2,1)}, u32[]{:S(2)}) copy-start(bf16[128,2560]{1,0:T(8,128)(2,1)} %param.8) | copy-start | bytes 1966084
  65.6 1.2 %copy-start.2 = (bf16[20,128,128]{2,1,0:T(8,128)(2,1)S(1)}, bf16[20,128,128]{2,1,0:T(8,128)(2,1)}, u32[]{:S(2)}) copy-start(bf16[20,128,128]{2,1,0:T(8,128)(2,1)} %get-tuple-element.9) | copy-start | bytes 1966084
  66.8 1.4 %copy-start.4 = (bf16[4,2,128,128]{3,2,1,0:T(8,128)(2,1)S(1)}, bf16[4,2,128,128]{3,2,1,0:T(8,128)(2,1)}, u32[]{:S(2)}) copy-start(bf16[4,2,128,128]{3,2,1,0:T(8,128)(2,1)} %get-tuple-element.10) | copy-start | bytes 786436
  66.8 2.5 %copy-start.3 = (bf16[4,2,128,128]{3,2,1,0:T(8,128)(2,1)S(1)}, bf16[4,2,128,128]{3,2,1,0:T(8,128)(2,1)}, u32[]{:S(2)}) copy-start(bf16[4,2,128,128]{3,2,1,0:T(8,128)(2,1)} %get-tuple-element.11) | copy-start | bytes 786436

commit v2 on v1

v2 whole, which is shorter than its diff:
```python
import functools
import math

import jax
import jax.numpy as jnp
from jax import lax
from jax.experimental import pallas as pl
from jax.experimental.pallas import tpu as pltpu
from jax.sharding import PartitionSpec as P

D = 128
T = 128
G = 5
KVH = 4
BLK = 2 * T
COLS = G * T
R = 2 * COLS
NP = 8
MASKED = -1e30
INV_ROOT = 1.0 / math.sqrt(D)
SCALE2 = INV_ROOT * math.log2(math.e)
BF = jnp.bfloat16
F32 = jnp.float32
MESH = pl.DeviceIdType.MESH


def dot(a, b, ca, cb):
    return lax.dot_general(a, b, (((ca,), (cb,)), ((), ())), preferred_element_type=F32)


STEP = 2
NI = NP // STEP
N = STEP * BLK
HALF = NI // 2
BACK = (0, 2, 1, 3, 5, 4, 6, 7)
LAST = {0: 0, 1: 1, 2: 2, 3: 3, 7: 4}


def kernel(lengths, prompt, resp, query, grad, oout, qout, rout, pout,
           pkv, rkv, live, kvb, xq, xg, xr, xl, sb, srb, eb, erb, mb, tp, lb, ot, fr, gp, dlt, dqt,
           osend, qsend, rf, rsend, pb, rb, rbf,
           st_s, st_r, loc, d_s, d_r, ag_s, ag_r, rs_s, rs_r, fin_s, fin_r, out_s, out_r):
    me = lax.axis_index("resp")
    z, x, c = me // 8, (me // 2) % 4, me % 2

    def device(p, core):
        dx = (0, 3, 1, 0, 3, 1, 2, 2)[p]
        zz = z if p in (0, 1, 2, 6) else 1 - z
        cc = c if core == 0 else 1 - c
        return zz * 8 + ((x + dx) % 4) * 2 + cc

    def remote(src, dst, ss, rs, to):
        return pltpu.make_async_remote_copy(
            src_ref=src, dst_ref=dst, send_sem=ss, recv_sem=rs, device_id={"resp": to}, device_id_type=MESH)

    barrier = pltpu.get_barrier_semaphore()
    peers = [(p, core) for p in (0, 1, 2, 3, 7) for core in (0, 1) if p or core]
    for p, core in peers:
        pl.semaphore_signal(barrier, inc=1, device_id={"resp": device(p, core)}, device_id_type=MESH)

    sib = device(0, 1)
    mine, other = 2 * c, 2 * (1 - c)
    rows = pl.ds(pl.multiple_of(c * T, T), T)
    orows = pl.ds(pl.multiple_of((1 - c) * T, T), T)
    W = 2 * G * D

    def columns(which):
        return pl.ds(pl.multiple_of(which * W, W), W)

    def by_head(src, dst):
        wide = src[...].astype(F32).reshape(T, 2, KVH * D).transpose(1, 0, 2).astype(BF)
        for h in range(KVH):
            for kv in (0, 1):
                dst[h, kv] = wide[kv, :, h * D:(h + 1) * D]

    by_head(prompt, pkv)
    live[...] = (lax.broadcasted_iota(jnp.int32, (16, T), 1) < lengths[0]).astype(F32).astype(BF)
    pl.semaphore_wait(barrier, len(peers))

    def direct(a, kv, p, core):
        head = (mine if core == 0 else other) + a
        return remote(pkv.at[head, kv], kvb.at[a, kv, BACK[p], rows, :],
                      d_s.at[a, kv, BACK[p], core], d_r.at[a, kv, BACK[p], core], device(p, core))

    near = (3, 1, 2)

    def direct_start(a, kv):
        for p in near:
            direct(a, kv, p, 0).start()
            direct(a, kv, p, 1).start()

    def exchange(k, src_other, src_mine, dst_other, dst_mine):
        away = remote(src_other, dst_other, st_s.at[k], st_r.at[k], sib)
        away.start()
        here = pltpu.make_async_copy(src_mine, dst_mine, loc.at[k])
        here.start()
        return away, here

    def exchange_wait(pair):
        pair[0].wait_recv()
        pair[1].wait()

    def heads_of(which):
        return pl.ds(which, 2)

    direct_start(0, 0)
    ex_q = exchange(0, query.at[:, columns(1 - c)], query.at[:, columns(c)], xq.at[1], xq.at[0])
    ex_kv = exchange(1, pkv.at[heads_of(other)], pkv.at[heads_of(mine)],
                     kvb.at[:, :, 0, rows, :], kvb.at[:, :, 0, rows, :])
    direct_start(0, 1)
    direct_start(1, 0)
    direct_start(1, 1)
    by_head(resp, rkv)
    ex_r = exchange(2, rkv.at[heads_of(other)], rkv.at[heads_of(mine)], xr.at[:, 1], xr.at[:, 0])
    ex_g = exchange(3, grad.at[:, columns(1 - c)], grad.at[:, columns(c)], xg.at[1], xg.at[0])
    ex_l = exchange(4, live, live, xl.at[1], xl.at[0])

    def ag(a, kv, kind):
        to = {3: 2, 4: 1, 5: 2, 6: 1, 7: 3}[kind]
        src = {3: 3, 4: 3, 5: 1, 6: 2, 7: 6}[kind]
        dst = {3: 4, 4: 5, 5: 6, 6: 6, 7: 7}[kind]
        part = {5: pl.ds(0, T), 6: pl.ds(T, T)}.get(kind, pl.ds(0, BLK))
        return remote(kvb.at[a, kv, src, part, :], kvb.at[a, kv, dst, part, :],
                      ag_s.at[a, kv, kind - 3], ag_r.at[a, kv, kind - 3], device(to, 0))

    def ag_second(a, kv):
        for p in near:
            direct(a, kv, BACK[p], 0).wait_recv()
            direct(a, kv, BACK[p], 1).wait_recv()
        for k in (5, 6, 3, 4):
            ag(a, kv, k).start()

    def ag_third(a, kv):
        ag(a, kv, 5).wait_recv()
        ag(a, kv, 6).wait_recv()
        ag(a, kv, 7).start()

    def ag_wait(a, kv, *kinds):
        for k in kinds:
            ag(a, kv, k).wait_recv()

    def rs(a, kind):
        to = {3: 1, 4: 2, 5: 1, 6: 2}[kind]
        src = {3: 4, 4: 5, 5: 6, 6: 6}[kind]
        part = {5: pl.ds(0, T), 6: pl.ds(T, T)}.get(kind, pl.ds(0, BLK))
        return remote(pb.at[a, :, src, part, :], rb.at[a, kind - 3, :, part, :],
                      rs_s.at[a, kind - 3], rs_r.at[a, kind - 3], device(to, 0))

    def rs_last(a, p, core):
        slot = LAST[BACK[p]]
        return remote(pb.at[a, :, p, rows if core == 0 else orows, :], rbf.at[a, slot, core],
                      fin_s.at[a, slot, core], fin_r.at[a, slot, core], device(p, core))

    def last_start(a, p):
        rs_last(a, p, 0).start()
        rs_last(a, p, 1).start()

    def sum_three(a):
        rs(a, 3).wait_recv()
        rs(a, 4).wait_recv()
        pb[a, :, 3] = (pb[a, :, 3].astype(F32) + rb[a, 0].astype(F32) + rb[a, 1].astype(F32)).astype(BF)
        last_start(a, 3)

    def sum_two(a):
        rs(a, 6).wait_recv()
        pb[a, :, 2, T:] = (pb[a, :, 2, T:].astype(F32) + rb[a, 3, :, T:].astype(F32)).astype(BF)
        last_start(a, 2)

    def sum_one(a):
        rs(a, 5).wait_recv()
        pb[a, :, 1, :T] = (pb[a, :, 1, :T].astype(F32) + rb[a, 2, :, :T].astype(F32)).astype(BF)
        last_start(a, 1)

    def rs_final(a):
        rs_last(a, 0, 1).wait_recv()
        for p in (1, 2, 3, 7):
            for core in (0, 1):
                rs_last(a, BACK[p], core).wait_recv()
        for core in (0, 1):
            total = pb[a, :, 0, rows, :] if core == 0 else rbf[a, 0, 1]
            total = total.astype(F32)
            for slot in (1, 2, 3, 4):
                total = total + rbf[a, slot, core].astype(F32)
            rf[(mine if core == 0 else other) + a, 1] = total.astype(BF)
        for h in (a, 2 + a):
            for kv in (0, 1):
                pout[:, kv, h * D:(h + 1) * D] = rf[h, 1, kv]

    def place(a):
        return pl.ds(pl.multiple_of((2 * c + a) * (G * D), G * D), G * D)

    def o_copy(a):
        return remote(osend.at[a], oout.at[:, place(a)], out_s.at[a, 0], out_r.at[a, 0], sib)

    def q_copy(a):
        return remote(qsend.at[a], qout.at[:, place(a)], out_s.at[a, 1], out_r.at[a, 1], sib)

    def r_copy(a):
        return remote(rsend.at[a], rf.at[2 * c + a, 0], out_s.at[a, 2], out_r.at[a, 2], sib)

    def at_step(i, hooks):
        for k, calls in hooks.items():
            @pl.when(i == k)
            def _():
                for call in calls:
                    call()

    def stacked(ref, a, b):
        return jnp.concatenate([ref[b, :, (a * G + g) * D:(a * G + g + 1) * D] for g in range(G)], axis=0)

    def queries_of(a):
        return jnp.concatenate([stacked(xq, a, 0), stacked(xq, a, 1)], axis=0)

    def fold(value, op):
        n = value.shape[0]
        return op(value.reshape(n // 8, 8, R), axis=0)

    def shard(a, kv, j):
        return kvb[a, kv, pl.ds(j * STEP, STEP)].reshape(N, D)

    def scores(a, half, hooks):
        def step(i, _):
            at_step(i, hooks)
            s = dot(shard(a, 0, half * HALF + i), queries_of(a), 1, 1)
            sb[i] = s
            mb[...] = jnp.maximum(mb[...], fold(s, jnp.max))
            return 0

        lax.fori_loop(0, HALF, step, 0)

    def weigh(a, half, hooks):
        def step(i, _):
            at_step(i, hooks)
            j = half * HALF + i
            e = jnp.exp2(sb[i] * SCALE2 - tp[a] * SCALE2)
            lb[a] += fold(e, jnp.sum)
            low = e.astype(BF)
            eb[a, j] = low
            ot[a] += dot(shard(a, 1, j), low, 0, 0)
            return 0

        lax.fori_loop(0, HALF, step, 0)

    def first_half(a, hooks_a, hooks_b, before_values):
        slot = lax.broadcasted_iota(jnp.int32, (T, G, T), 2).reshape(T, COLS)
        key = lax.broadcasted_iota(jnp.int32, (T, COLS), 0)
        for b in (0, 1):
            s = dot(xr[a, b, 0], stacked(xq, a, b), 1, 1)
            srb[:, b * COLS:(b + 1) * COLS] = jnp.where(key <= slot, s, MASKED)
        mb[...] = fold(srb[...], jnp.max)
        scores(a, 0, hooks_a)
        tp[a] = jnp.max(mb[...], axis=0, keepdims=True)
        er = jnp.exp2(srb[...] * SCALE2 - tp[a] * SCALE2)
        lb[a] = fold(er, jnp.sum)
        erb[a] = er.astype(BF)
        for b in (0, 1):
            cols = slice(b * COLS, (b + 1) * COLS)
            ot[a, :, cols] = dot(xr[a, b, 1], erb[a, :, cols], 0, 0)
        before_values()
        weigh(a, 0, hooks_b)

    def second_half(a, hooks_a, hooks_b):
        mb[...] = jnp.broadcast_to(tp[a], (8, R))
        scores(a, 1, hooks_a)
        top = jnp.max(mb[...], axis=0, keepdims=True)
        shrink = jnp.exp2((tp[a] - top) * SCALE2)
        tp[a] = top
        fr[a] = shrink
        lb[a] = lb[a] * shrink
        ot[a] = ot[a] * shrink
        weigh(a, 1, hooks_b)

    def rowwise(a):
        inv = 1.0 / jnp.sum(lb[a], axis=0, keepdims=True)
        for b in (0, 1):
            on = xl[b, 0:1, :].astype(F32) > 0.0
            for g in range(G):
                lo = b * COLS + g * T
                cols = slice(lo, lo + T)
                hd = slice((a * G + g) * D, (a * G + g + 1) * D)
                att = ot[a, :, cols] * inv[:, cols]
                gt = jnp.where(on, xg[b, :, hd].astype(F32).T, 0.0)
                delta = jnp.sum(gt * att, axis=0, keepdims=True) * inv[:, cols]
                gt = gt * inv[:, cols]
                shrink = fr[a, :, cols]
                dlt[a, 0, :, cols] = delta * shrink
                dlt[a, 1, :, cols] = delta
                gp[a, 0, cols, :] = (gt * shrink).T.astype(BF)
                gp[a, 1, cols, :] = gt.T.astype(BF)
                att = jnp.where(on, att, 0.0).T.astype(BF)
                if b == 0:
                    oout[:, pl.ds(pl.multiple_of((2 * c + a) * (G * D) + g * D, D), D)] = att
                else:
                    osend[a, :, g * D:(g + 1) * D] = att
        o_copy(a).start()

    def backward(a, half, ends, start):
        def step(i, _):
            j = HALF + i if half else HALF - 1 - i
            ps = pl.ds(j * STEP, STEP)
            scaled = gp[a, half]
            dp = dot(shard(a, 1, j), scaled, 1, 1) - dlt[a, half]
            ds = (eb[a, j].astype(F32) * dp).astype(BF)
            pb[a, 1, ps] = dot(eb[a, j], scaled, 1, 0).astype(BF).reshape(STEP, BLK, D)
            pb[a, 0, ps] = (dot(ds, queries_of(a), 1, 0) * INV_ROOT).astype(BF).reshape(STEP, BLK, D)
            dqt[a] += dot(shard(a, 0, j), ds, 0, 0)
            at_step(i, ends)
            return 0

        if start:
            dqt[a] = jnp.zeros((D, R), F32)
        lax.fori_loop(0, HALF, step, 0)

    def backward_own(a):
        for b in (0, 1):
            cols = slice(b * COLS, (b + 1) * COLS)
            dp = dot(xr[a, b, 1], gp[a, 0, cols, :], 1, 1) - dlt[a, 0, :, cols]
            ds = (erb[a, :, cols].astype(F32) * dp).astype(BF)
            dv = dot(erb[a, :, cols], gp[a, 0, cols, :], 1, 0).astype(BF)
            dk = (dot(ds, stacked(xq, a, b), 1, 0) * INV_ROOT).astype(BF)
            dqt[a, :, cols] += dot(xr[a, b, 0], ds, 0, 0)
            if b == 0:
                rf[2 * c + a, 0, 0] = dk
                rf[2 * c + a, 0, 1] = dv
            else:
                rsend[a, 0] = dk
                rsend[a, 1] = dv
        r_copy(a).start()
        for b in (0, 1):
            for g in range(G):
                lo = b * COLS + g * T
                got = (dqt[a, :, lo:lo + T] * INV_ROOT).T.astype(BF)
                if b == 0:
                    qout[:, pl.ds(pl.multiple_of((2 * c + a) * (G * D) + g * D, D), D)] = got
                else:
                    qsend[a, :, g * D:(g + 1) * D] = got
        q_copy(a).start()

    f = functools.partial

    def far_ends(a):
        return {0: [rs(a, 3).start, rs(a, 4).start], 1: [rs(a, 5).start, rs(a, 6).start, f(last_start, a, 7)]}

    def near_ends(a):
        return {0: [f(sum_three, a), f(sum_two, a)], 1: [f(sum_one, a), rs_last(a, 0, 1).start]}

    for pair in (ex_q, ex_r, ex_kv):
        exchange_wait(pair)
    first_half(0, {0: [f(ag_second, 0, 0)]}, {}, f(ag_second, 0, 1))
    first_half(1, {0: [f(ag_second, 1, 0)]}, {0: [f(ag_third, 0, 0)]}, f(ag_second, 1, 1))
    second_half(0, {0: [f(ag_wait, 0, 0, 3, 4)], 1: [f(ag_third, 0, 1), f(ag_wait, 0, 0, 7)]},
                {0: [f(ag_third, 1, 0), f(ag_wait, 0, 1, 3, 4)], 1: [f(ag_third, 1, 1), f(ag_wait, 0, 1, 7)]})
    exchange_wait(ex_g)
    exchange_wait(ex_l)
    rowwise(0)
    backward(0, 1, far_ends(0), True)
    second_half(1, {0: [f(ag_wait, 1, 0, 3, 4)], 1: [f(ag_wait, 1, 0, 7)]},
                {0: [f(ag_wait, 1, 1, 3, 4)], 1: [f(ag_wait, 1, 1, 7)]})
    rowwise(1)
    backward(1, 1, far_ends(1), True)
    backward(0, 0, near_ends(0), False)
    backward(1, 0, near_ends(1), False)
    backward_own(0)
    backward_own(1)
    rs_final(0)
    r_copy(0).wait()
    r_copy(1).wait()
    for h in range(KVH):
        for kv in (0, 1):
            rout[:, kv, h * D:(h + 1) * D] = rf[h, 0, kv]
    rs_final(1)

    for away, _ in (ex_q, ex_kv, ex_r, ex_g, ex_l):
        away.wait_send()
    for a in (0, 1):
        for kv in (0, 1):
            for p in near:
                direct(a, kv, p, 0).wait_send()
                direct(a, kv, p, 1).wait_send()
            for kind in range(3, 8):
                ag(a, kv, kind).wait_send()
        for kind in range(3, 7):
            rs(a, kind).wait_send()
        rs_last(a, 0, 1).wait_send()
        for p in (1, 2, 3, 7):
            rs_last(a, p, 0).wait_send()
            rs_last(a, p, 1).wait_send()
        o_copy(a).wait()
        q_copy(a).wait()


def per_device(prompt_kv, queries, response_key_values, grad_out, lengths):
    vmem = pl.BlockSpec(memory_space=pltpu.VMEM)
    dma = pltpu.SemaphoreType.DMA
    flops = 6 * 2 * 2 * R * (NP * BLK + T) * D
    return pl.pallas_call(
        kernel,
        out_shape=(
            jax.ShapeDtypeStruct(queries.shape, BF),
            jax.ShapeDtypeStruct(queries.shape, BF),
            jax.ShapeDtypeStruct(prompt_kv.shape, BF),
            jax.ShapeDtypeStruct(prompt_kv.shape, BF),
        ),
        in_specs=[pl.BlockSpec(memory_space=pltpu.SMEM)] + [vmem] * 4,
        out_specs=(vmem,) * 4,
        scratch_shapes=[
            pltpu.VMEM((KVH, 2, T, D), BF),
            pltpu.VMEM((KVH, 2, T, D), BF),
            pltpu.VMEM((16, T), BF),
            pltpu.VMEM((2, 2, NP, BLK, D), BF),
            pltpu.VMEM((2, T, 2 * G * D), BF),
            pltpu.VMEM((2, T, 2 * G * D), BF),
            pltpu.VMEM((2, 2, 2, T, D), BF),
            pltpu.VMEM((2, 16, T), BF),
            pltpu.VMEM((HALF, N, R), F32),
            pltpu.VMEM((T, R), F32),
            pltpu.VMEM((2, NI, N, R), BF),
            pltpu.VMEM((2, T, R), BF),
            pltpu.VMEM((8, R), F32),
            pltpu.VMEM((2, 1, R), F32),
            pltpu.VMEM((2, 8, R), F32),
            pltpu.VMEM((2, D, R), F32),
            pltpu.VMEM((2, 1, R), F32),
            pltpu.VMEM((2, 2, R, D), BF),
            pltpu.VMEM((2, 2, 1, R), F32),
            pltpu.VMEM((2, D, R), F32),
            pltpu.VMEM((2, T, G * D), BF),
            pltpu.VMEM((2, T, G * D), BF),
            pltpu.VMEM((KVH, 2, 2, T, D), BF),
            pltpu.VMEM((2, 2, T, D), BF),
            pltpu.VMEM((2, 2, NP, BLK, D), BF),
            pltpu.VMEM((2, 4, 2, BLK, D), BF),
            pltpu.VMEM((2, 5, 2, 2, T, D), BF),
            dma((5,)), dma((5,)), dma((5,)),
            dma((2, 2, 4, 2)), dma((2, 2, 4, 2)),
            dma((2, 2, 5)), dma((2, 2, 5)),
            dma((2, 4)), dma((2, 4)),
            dma((2, 5, 2)), dma((2, 5, 2)),
            dma((2, 3)), dma((2, 3)),
        ],
        compiler_params=pltpu.CompilerParams(
            collective_id=0, has_side_effects=True, vmem_limit_bytes=56 << 20),
        cost_estimate=pl.CostEstimate(flops=flops, bytes_accessed=8 << 20, transcendentals=2 * R * (NP * BLK + T)),
        name="shared_prompt_attention",
    )(lengths, prompt_kv, response_key_values, queries, grad_out)


def solution(mesh):
    wide, thick = P(("grp", "resp"), None), P(("grp", "resp"), None, None)
    return jax.shard_map(
        per_device,
        mesh=mesh,
        in_specs=(thick, wide, thick, wide, P(("grp", "resp"))),
        out_specs=(wide, wide, thick, thick),
        check_vma=False,
    )
```

time: 71.1 us -> 56.8 us (0.80)
  Pallas kernels: 56.5 us -> 50.4 us
  local copies, waits for them, and re-layouts: 10.9 us -> 4.87 us
  other arithmetic: 1.49 us -> 0 us
    pallas_call x1, Pallas kernels: 56.5 us -> 50.4 us  [per_device(): pl.pallas_call(kernel, out_shape=(jax.ShapeDtypeStruct(queries.shape, BF)...]
    unnamed x18 -> x10, local copies, waits for them, and re-layouts: 7.13 us -> 4.87 us
    transpose x4 -> x0, local copies, waits for them, and re-layouts: 2.09 us -> none  [the longest x2 1.74 us: per_device(): flat = lambda v: v.transpose(1, 0, 2).reshape(T, KVH * G * D)]
    reshape x4 -> x0, local copies, waits for them, and re-layouts: 1.7 us -> none  [the longest x1 0.85 us: per_device(): pkv = prompt_kv.reshape(T, 2, KVH, D).transpose(2, 1, 0, 3)]
    concatenate x1 -> x0, other arithmetic: 1.35 us -> none  [per_device(): pack = jnp.concatenate([by_head(queries), by_head(grads), rkv], axis=1)]
where the time goes in v2:
time: 56.8 us; the launch traced here: 56.6 us
  Pallas kernels  50.4 us (89%)
  local copies, waits for them, and re-layouts  4.87 us (9%)
  between operations  1.3 us (2%)
    pallas_call x1, Pallas kernels, per_device(): pl.pallas_call(kernel, out_shape=(jax.ShapeDtypeStruct(queries.shape, BF)...  50.4 us
    unnamed x10, local copies, waits for them, and re-layouts  4.87 us

profile of v2, /device:TPU:1, one launch (start us, length us, event | category | flops | bytes accessed | tf_op | source)
XLA Modules:
  0.0 56.6 jit_solution(15767273160808152090)
XLA Ops:
  1.3 50.4 %shared_prompt_attention.1 = (bf16[128,2560]{1,0:T(8,128)(2,1)}, bf16[128,2560]{1,0:T(8,128)(2,1)}, bf16[128,2,512]{2,1,0:T(2,128)(2,1)}, bf16[128,2,512]{2,1,0:T(2,128)(2,1)}) custom-call(s32[1]{0:T(128)S(6)} %copy.13.lengths, bf16[128,2,512]{2,1,0:T(2,128)(2,1)} %prompt.1, bf16[128,2,512]{2,1,0:T(2,128)(2,1)} %resp.1, bf16[128,2560]{1,0:T(8,128)(2,1)} %query.1, ...), custom_call_target="tpu_custom_call" | custom-call | flops 8556380160 | bytes 8388608 | tf_op jit(solution)/shard_map/shared_prompt_attention/pallas_call | solution.py:396
  51.7 0.0 copy-start
  51.7 2.0 %copy.14 = bf16[128,2560]{1,0:T(8,128)(2,1)} copy(bf16[128,2560]{1,0:T(8,128)(2,1)} %get-tuple-element.8) | data formatting | bytes 1310720
  53.7 0.0 copy-done
  53.7 0.0 copy-start.2
  53.8 0.8 %copy.15 = bf16[128,2560]{1,0:T(8,128)(2,1)} copy(bf16[128,2560]{1,0:T(8,128)(2,1)S(1)} %copy-done) | data formatting | bytes 1310720
  54.6 0.3 copy-done.2
  54.8 0.0 copy-start.1
  54.8 0.7 %copy.16 = bf16[128,2,512]{2,1,0:T(2,128)(2,1)} copy(bf16[128,2,512]{2,1,0:T(2,128)(2,1)S(1)} %copy-done.2) | data formatting | bytes 524288
  55.5 0.3 copy-done.1
  55.9 0.7 %copy.17 = bf16[128,2,512]{2,1,0:T(2,128)(2,1)} copy(bf16[128,2,512]{2,1,0:T(2,128)(2,1)S(1)} %copy-done.1) | data formatting | bytes 524288
Async XLA Ops:
  51.7 2.0 %copy-start = (bf16[128,2560]{1,0:T(8,128)(2,1)S(1)}, bf16[128,2560]{1,0:T(8,128)(2,1)}, u32[]{:S(2)}) copy-start(bf16[128,2560]{1,0:T(8,128)(2,1)} %get-tuple-element.9) | copy-start | bytes 1966084
  53.7 1.1 %copy-start.2 = (bf16[128,2,512]{2,1,0:T(2,128)(2,1)S(1)}, bf16[128,2,512]{2,1,0:T(2,128)(2,1)}, u32[]{:S(2)}) copy-start(bf16[128,2,512]{2,1,0:T(2,128)(2,1)} %get-tuple-element.10) | copy-start | bytes 786436
  54.8 1.0 %copy-start.1 = (bf16[128,2,512]{2,1,0:T(2,128)(2,1)S(1)}, bf16[128,2,512]{2,1,0:T(2,128)(2,1)}, u32[]{:S(2)}) copy-start(bf16[128,2,512]{2,1,0:T(2,128)(2,1)} %get-tuple-element.11) | copy-start | bytes 786436

commit v3 on v2

--- a/solution.py
+++ b/solution.py
@@ -39,7 +39,7 @@
 def kernel(lengths, prompt, resp, query, grad, oout, qout, rout, pout,
            pkv, rkv, live, kvb, xq, xg, xr, xl, sb, srb, eb, erb, mb, tp, lb, ot, fr, gp, dlt, dqt,
            osend, qsend, rf, rsend, pb, rb, rbf,
-           st_s, st_r, loc, d_s, d_r, ag_s, ag_r, rs_s, rs_r, fin_s, fin_r, out_s, out_r):
+           st_s, st_r, loc, d_s, d_r, ag_s, ag_r, rs_s, rs_r, fin_s, fin_r, out_s, out_r, own):
     me = lax.axis_index("resp")
     z, x, c = me // 8, (me // 2) % 4, me % 2
 
@@ -190,10 +190,16 @@
         return pl.ds(pl.multiple_of((2 * c + a) * (G * D), G * D), G * D)
 
     def o_copy(a):
-        return remote(osend.at[a], oout.at[:, place(a)], out_s.at[a, 0], out_r.at[a, 0], sib)
+        return remote(osend.at[a, 1], oout.at[:, place(a)], out_s.at[a, 0], out_r.at[a, 0], sib)
 
     def q_copy(a):
-        return remote(qsend.at[a], qout.at[:, place(a)], out_s.at[a, 1], out_r.at[a, 1], sib)
+        return remote(qsend.at[a, 1], qout.at[:, place(a)], out_s.at[a, 1], out_r.at[a, 1], sib)
+
+    def o_own(a):
+        return pltpu.make_async_copy(osend.at[a, 0], oout.at[:, place(a)], own.at[a, 0])
+
+    def q_own(a):
+        return pltpu.make_async_copy(qsend.at[a, 0], qout.at[:, place(a)], own.at[a, 1])
 
     def r_copy(a):
         return remote(rsend.at[a], rf.at[2 * c + a, 0], out_s.at[a, 2], out_r.at[a, 2], sib)
@@ -288,11 +294,9 @@
                 gp[a, 0, cols, :] = (gt * shrink).T.astype(BF)
                 gp[a, 1, cols, :] = gt.T.astype(BF)
                 att = jnp.where(on, att, 0.0).T.astype(BF)
-                if b == 0:
-                    oout[:, pl.ds(pl.multiple_of((2 * c + a) * (G * D) + g * D, D), D)] = att
-                else:
-                    osend[a, :, g * D:(g + 1) * D] = att
+                osend[a, b, :, g * D:(g + 1) * D] = att
         o_copy(a).start()
+        o_own(a).start()
 
     def backward(a, half, ends, start):
         def step(i, _):
@@ -330,11 +334,9 @@
             for g in range(G):
                 lo = b * COLS + g * T
                 got = (dqt[a, :, lo:lo + T] * INV_ROOT).T.astype(BF)
-                if b == 0:
-                    qout[:, pl.ds(pl.multiple_of((2 * c + a) * (G * D) + g * D, D), D)] = got
-                else:
-                    qsend[a, :, g * D:(g + 1) * D] = got
+                qsend[a, b, :, g * D:(g + 1) * D] = got
         q_copy(a).start()
+        q_own(a).start()
 
     f = functools.partial
 
@@ -387,13 +389,29 @@
             rs_last(a, p, 1).wait_send()
         o_copy(a).wait()
         q_copy(a).wait()
+        o_own(a).wait()
+        q_own(a).wait()
+
+
+def hand_over(*refs):
+    sources, targets, staged, sems = refs[:4], refs[4:8], refs[8:12], refs[12]
+    arrive = [pltpu.make_async_copy(sources[k], staged[k], sems.at[0, k]) for k in range(4)]
+    leave = [pltpu.make_async_copy(staged[k], targets[k], sems.at[1, k]) for k in range(4)]
+    for copy in arrive:
+        copy.start()
+    for k in range(4):
+        arrive[k].wait()
+        leave[k].start()
+    for copy in leave:
+        copy.wait()
 
 
 def per_device(prompt_kv, queries, response_key_values, grad_out, lengths):
     vmem = pl.BlockSpec(memory_space=pltpu.VMEM)
+    anywhere = pl.BlockSpec(memory_space=pl.ANY)
     dma = pltpu.SemaphoreType.DMA
     flops = 6 * 2 * 2 * R * (NP * BLK + T) * D
-    return pl.pallas_call(
+    found = pl.pallas_call(
         kernel,
         out_shape=(
             jax.ShapeDtypeStruct(queries.shape, BF),
@@ -401,8 +419,8 @@
             jax.ShapeDtypeStruct(prompt_kv.shape, BF),
             jax.ShapeDtypeStruct(prompt_kv.shape, BF),
         ),
-        in_specs=[pl.BlockSpec(memory_space=pltpu.SMEM)] + [vmem] * 4,
-        out_specs=(vmem,) * 4,
+        in_specs=[pl.BlockSpec(memory_space=pltpu.SMEM), vmem, vmem, anywhere, anywhere],
+        out_specs=(anywhere, anywhere, vmem, vmem),
         scratch_shapes=[
             pltpu.VMEM((KVH, 2, T, D), BF),
             pltpu.VMEM((KVH, 2, T, D), BF),
@@ -424,8 +442,8 @@
             pltpu.VMEM((2, 2, R, D), BF),
             pltpu.VMEM((2, 2, 1, R), F32),
             pltpu.VMEM((2, D, R), F32),
-            pltpu.VMEM((2, T, G * D), BF),
-            pltpu.VMEM((2, T, G * D), BF),
+            pltpu.VMEM((2, 2, T, G * D), BF),
+            pltpu.VMEM((2, 2, T, G * D), BF),
             pltpu.VMEM((KVH, 2, 2, T, D), BF),
             pltpu.VMEM((2, 2, T, D), BF),
             pltpu.VMEM((2, 2, NP, BLK, D), BF),
@@ -436,13 +454,21 @@
             dma((2, 2, 5)), dma((2, 2, 5)),
             dma((2, 4)), dma((2, 4)),
             dma((2, 5, 2)), dma((2, 5, 2)),
-            dma((2, 3)), dma((2, 3)),
+            dma((2, 3)), dma((2, 3)), dma((2, 2)),
         ],
         compiler_params=pltpu.CompilerParams(
             collective_id=0, has_side_effects=True, vmem_limit_bytes=56 << 20),
         cost_estimate=pl.CostEstimate(flops=flops, bytes_accessed=8 << 20, transcendentals=2 * R * (NP * BLK + T)),
         name="shared_prompt_attention",
     )(lengths, prompt_kv, response_key_values, queries, grad_out)
+    return pl.pallas_call(
+        hand_over,
+        out_shape=tuple(jax.ShapeDtypeStruct(v.shape, v.dtype) for v in found),
+        in_specs=[anywhere] * 4,
+        out_specs=(anywhere,) * 4,
+        scratch_shapes=[pltpu.VMEM(v.shape, v.dtype) for v in found] + [dma((2, 4))],
+        name="hand_over",
+    )(*found)
 
 
 def solution(mesh):

time: 56.8 us -> 53.6 us (0.944)
  local copies, waits for them, and re-layouts: 4.87 us -> 0 us
  Pallas kernels: 50.4 us -> 52 us
    unnamed x10 -> x0, local copies, waits for them, and re-layouts: 4.87 us -> none
    pallas_call x0 -> x1, Pallas kernels: none -> 2.38 us  [per_device(): pl.pallas_call(hand_over, out_shape=tuple((jax.ShapeDtypeStruct(v.shape,...]
    pallas_call x1, Pallas kernels: 50.4 us -> 49.6 us  [per_device(): pl.pallas_call(kernel, out_shape=(jax.ShapeDtypeStruct(queries.shape, BF)...]
where the time goes in v3:
time: 53.6 us; the launch traced here: 53.4 us
  Pallas kernels  52 us (97%)
  between operations  1.45 us (3%)
    pallas_call x1, Pallas kernels, per_device(): pl.pallas_call(kernel, out_shape=(jax.ShapeDtypeStruct(queries.shape, BF)...  49.6 us
    pallas_call x1, Pallas kernels, per_device(): pl.pallas_call(hand_over, out_shape=tuple((jax.ShapeDtypeStruct(v.shape,...  2.38 us

profile of v3, /device:TPU:1, one launch (start us, length us, event | category | flops | bytes accessed | tf_op | source)
XLA Modules:
  0.0 53.4 jit_solution(6927048559603004675)
XLA Ops:
  1.3 49.6 %shared_prompt_attention.1 = (bf16[128,2560]{1,0:T(8,128)(2,1)}, bf16[128,2560]{1,0:T(8,128)(2,1)}, bf16[128,2,512]{2,1,0:T(2,128)(2,1)}, bf16[128,2,512]{2,1,0:T(2,128)(2,1)}) custom-call(s32[1]{0:T(128)S(6)} %copy.9.lengths, bf16[128,2,512]{2,1,0:T(2,128)(2,1)} %prompt.1, bf16[128,2,512]{2,1,0:T(2,128)(2,1)} %resp.1, bf16[128,2560]{1,0:T(8,128)(2,1)} %query.1, ...), custom_call_target="tpu_custom_call" | custom-call | flops 8556380160 | bytes 8388608 | tf_op jit(solution)/shard_map/shared_prompt_attention/pallas_call | solution.py:414
  50.9 2.4 %hand_over.1 = (bf16[128,2560]{1,0:T(8,128)(2,1)}, bf16[128,2560]{1,0:T(8,128)(2,1)}, bf16[128,2,512]{2,1,0:T(2,128)(2,1)}, bf16[128,2,512]{2,1,0:T(2,128)(2,1)}) custom-call(bf16[128,2560]{1,0:T(8,128)(2,1)} %get-tuple-element.8.refs_0_, bf16[128,2560]{1,0:T(8,128)(2,1)} %get-tuple-element.9.refs_1_, bf16[128,2,512]{2,1,0:T(2,128)(2,1)} %get-tuple-element.10.refs_2_, ...), custom_call_target="tpu_custom_call" | custom-call | tf_op jit(solution)/shard_map/hand_over/pallas_call | solution.py:464

commit v4 on v3

--- a/solution.py
+++ b/solution.py
@@ -224,57 +224,62 @@
     def shard(a, kv, j):
         return kvb[a, kv, pl.ds(j * STEP, STEP)].reshape(N, D)
 
-    def scores(a, half, hooks):
+    def loop(hooks, works, ends=None):
         def step(i, _):
             at_step(i, hooks)
+            for work in works:
+                work(i)
+            at_step(i, ends or {})
+            return 0
+
+        lax.fori_loop(0, HALF, step, 0)
+
+    def scores(a, half):
+        def work(i):
             s = dot(shard(a, 0, half * HALF + i), queries_of(a), 1, 1)
-            sb[i] = s
-            mb[...] = jnp.maximum(mb[...], fold(s, jnp.max))
-            return 0
-
-        lax.fori_loop(0, HALF, step, 0)
-
-    def weigh(a, half, hooks):
-        def step(i, _):
-            at_step(i, hooks)
+            sb[a, i] = s
+            mb[a] = jnp.maximum(mb[a], fold(s, jnp.max))
+
+        return work
+
+    def weigh(a, half):
+        def work(i):
             j = half * HALF + i
-            e = jnp.exp2(sb[i] * SCALE2 - tp[a] * SCALE2)
+            e = jnp.exp2(sb[a, i] * SCALE2 - tp[a] * SCALE2)
             lb[a] += fold(e, jnp.sum)
             low = e.astype(BF)
             eb[a, j] = low
             ot[a] += dot(shard(a, 1, j), low, 0, 0)
-            return 0
-
-        lax.fori_loop(0, HALF, step, 0)
-
-    def first_half(a, hooks_a, hooks_b, before_values):
+
+        return work
+
+    def own_scores(a):
         slot = lax.broadcasted_iota(jnp.int32, (T, G, T), 2).reshape(T, COLS)
         key = lax.broadcasted_iota(jnp.int32, (T, COLS), 0)
         for b in (0, 1):
             s = dot(xr[a, b, 0], stacked(xq, a, b), 1, 1)
-            srb[:, b * COLS:(b + 1) * COLS] = jnp.where(key <= slot, s, MASKED)
-        mb[...] = fold(srb[...], jnp.max)
-        scores(a, 0, hooks_a)
-        tp[a] = jnp.max(mb[...], axis=0, keepdims=True)
-        er = jnp.exp2(srb[...] * SCALE2 - tp[a] * SCALE2)
+            srb[a, :, b * COLS:(b + 1) * COLS] = jnp.where(key <= slot, s, MASKED)
+        mb[a] = fold(srb[a], jnp.max)
+
+    def own_weights(a):
+        tp[a] = jnp.max(mb[a], axis=0, keepdims=True)
+        er = jnp.exp2(srb[a] * SCALE2 - tp[a] * SCALE2)
         lb[a] = fold(er, jnp.sum)
         erb[a] = er.astype(BF)
         for b in (0, 1):
             cols = slice(b * COLS, (b + 1) * COLS)
             ot[a, :, cols] = dot(xr[a, b, 1], erb[a, :, cols], 0, 0)
-        before_values()
-        weigh(a, 0, hooks_b)
-
-    def second_half(a, hooks_a, hooks_b):
-        mb[...] = jnp.broadcast_to(tp[a], (8, R))
-        scores(a, 1, hooks_a)
-        top = jnp.max(mb[...], axis=0, keepdims=True)
+
+    def grown(a):
+        mb[a] = jnp.broadcast_to(tp[a], (8, R))
+
+    def shrink_first(a):
+        top = jnp.max(mb[a], axis=0, keepdims=True)
         shrink = jnp.exp2((tp[a] - top) * SCALE2)
         tp[a] = top
         fr[a] = shrink
         lb[a] = lb[a] * shrink
         ot[a] = ot[a] * shrink
-        weigh(a, 1, hooks_b)
 
     def rowwise(a):
         inv = 1.0 / jnp.sum(lb[a], axis=0, keepdims=True)
@@ -298,8 +303,8 @@
         o_copy(a).start()
         o_own(a).start()
 
-    def backward(a, half, ends, start):
-        def step(i, _):
+    def backward(a, half):
+        def work(i):
             j = HALF + i if half else HALF - 1 - i
             ps = pl.ds(j * STEP, STEP)
             scaled = gp[a, half]
@@ -308,12 +313,8 @@
             pb[a, 1, ps] = dot(eb[a, j], scaled, 1, 0).astype(BF).reshape(STEP, BLK, D)
             pb[a, 0, ps] = (dot(ds, queries_of(a), 1, 0) * INV_ROOT).astype(BF).reshape(STEP, BLK, D)
             dqt[a] += dot(shard(a, 0, j), ds, 0, 0)
-            at_step(i, ends)
-            return 0
-
-        if start:
-            dqt[a] = jnp.zeros((D, R), F32)
-        lax.fori_loop(0, HALF, step, 0)
+
+        return work
 
     def backward_own(a):
         for b in (0, 1):
@@ -348,20 +349,31 @@
 
     for pair in (ex_q, ex_r, ex_kv):
         exchange_wait(pair)
-    first_half(0, {0: [f(ag_second, 0, 0)]}, {}, f(ag_second, 0, 1))
-    first_half(1, {0: [f(ag_second, 1, 0)]}, {0: [f(ag_third, 0, 0)]}, f(ag_second, 1, 1))
-    second_half(0, {0: [f(ag_wait, 0, 0, 3, 4)], 1: [f(ag_third, 0, 1), f(ag_wait, 0, 0, 7)]},
-                {0: [f(ag_third, 1, 0), f(ag_wait, 0, 1, 3, 4)], 1: [f(ag_third, 1, 1), f(ag_wait, 0, 1, 7)]})
+    for a in (0, 1):
+        dqt[a] = jnp.zeros((D, R), F32)
+    own_scores(0)
+    loop({0: [f(ag_second, 0, 0)]}, [scores(0, 0)])
+    own_weights(0)
+    own_scores(1)
+    loop({0: [f(ag_second, 0, 1), f(ag_second, 1, 0)]}, [weigh(0, 0), scores(1, 0)])
+    own_weights(1)
+    loop({0: [f(ag_second, 1, 1)], 1: [f(ag_third, 0, 0)]}, [weigh(1, 0)])
+    grown(0)
+    loop({0: [f(ag_wait, 0, 0, 3, 4)], 1: [f(ag_third, 0, 1), f(ag_wait, 0, 0, 7)]}, [scores(0, 1)])
+    shrink_first(0)
+    loop({0: [f(ag_wait, 0, 1, 3, 4)], 1: [f(ag_wait, 0, 1, 7)]}, [weigh(0, 1)])
     exchange_wait(ex_g)
     exchange_wait(ex_l)
     rowwise(0)
-    backward(0, 1, far_ends(0), True)
-    second_half(1, {0: [f(ag_wait, 1, 0, 3, 4)], 1: [f(ag_wait, 1, 0, 7)]},
-                {0: [f(ag_wait, 1, 1, 3, 4)], 1: [f(ag_wait, 1, 1, 7)]})
+    loop({0: [f(ag_third, 1, 0)], 1: [f(ag_third, 1, 1)]}, [backward(0, 1)], far_ends(0))
+    grown(1)
+    loop({0: [f(ag_wait, 1, 0, 3, 4)], 1: [f(ag_wait, 1, 0, 7)]}, [scores(1, 1)])
+    shrink_first(1)
+    loop({0: [f(ag_wait, 1, 1, 3, 4)], 1: [f(ag_wait, 1, 1, 7)]}, [weigh(1, 1)])
     rowwise(1)
-    backward(1, 1, far_ends(1), True)
-    backward(0, 0, near_ends(0), False)
-    backward(1, 0, near_ends(1), False)
+    loop({}, [backward(1, 1)], far_ends(1))
+    loop({}, [backward(0, 0)], near_ends(0))
+    loop({}, [backward(1, 0)], near_ends(1))
     backward_own(0)
     backward_own(1)
     rs_final(0)
@@ -430,11 +442,11 @@
             pltpu.VMEM((2, T, 2 * G * D), BF),
             pltpu.VMEM((2, 2, 2, T, D), BF),
             pltpu.VMEM((2, 16, T), BF),
-            pltpu.VMEM((HALF, N, R), F32),
-            pltpu.VMEM((T, R), F32),
+            pltpu.VMEM((2, HALF, N, R), F32),
+            pltpu.VMEM((2, T, R), F32),
             pltpu.VMEM((2, NI, N, R), BF),
             pltpu.VMEM((2, T, R), BF),
-            pltpu.VMEM((8, R), F32),
+            pltpu.VMEM((2, 8, R), F32),
             pltpu.VMEM((2, 1, R), F32),
             pltpu.VMEM((2, 8, R), F32),
             pltpu.VMEM((2, D, R), F32),
@@ -457,7 +469,7 @@
             dma((2, 3)), dma((2, 3)), dma((2, 2)),
         ],
         compiler_params=pltpu.CompilerParams(
-            collective_id=0, has_side_effects=True, vmem_limit_bytes=56 << 20),
+            collective_id=0, has_side_effects=True, vmem_limit_bytes=60 << 20),
         cost_estimate=pl.CostEstimate(flops=flops, bytes_accessed=8 << 20, transcendentals=2 * R * (NP * BLK + T)),
         name="shared_prompt_attention",
     )(lengths, prompt_kv, response_key_values, queries, grad_out)

time: 53.6 us -> 53 us (0.989)
  Pallas kernels: 52 us -> 51.4 us
    pallas_call x1, Pallas kernels: 49.6 us -> 49 us  [per_device(): pl.pallas_call(kernel, out_shape=(jax.ShapeDtypeStruct(queries.shape, BF)...]
where the time goes in v4:
time: 53 us; the launch traced here: 52.8 us
  Pallas kernels  51.4 us (97%)
  between operations  1.45 us (3%)
    pallas_call x1, Pallas kernels, per_device(): pl.pallas_call(kernel, out_shape=(jax.ShapeDtypeStruct(queries.shape, BF)...  49 us
    pallas_call x1, Pallas kernels, per_device(): pl.pallas_call(hand_over, out_shape=tuple((jax.ShapeDtypeStruct(v.shape,...  2.38 us

profile of v4, /device:TPU:1, one launch (start us, length us, event | category | flops | bytes accessed | tf_op | source)
XLA Modules:
  0.0 52.8 jit_solution(8301881359141123059)
XLA Ops:
  1.3 49.0 %shared_prompt_attention.1 = (bf16[128,2560]{1,0:T(8,128)(2,1)}, bf16[128,2560]{1,0:T(8,128)(2,1)}, bf16[128,2,512]{2,1,0:T(2,128)(2,1)}, bf16[128,2,512]{2,1,0:T(2,128)(2,1)}) custom-call(s32[1]{0:T(128)S(6)} %copy.9.lengths, bf16[128,2,512]{2,1,0:T(2,128)(2,1)} %prompt.1, bf16[128,2,512]{2,1,0:T(2,128)(2,1)} %resp.1, bf16[128,2560]{1,0:T(8,128)(2,1)} %query.1, ...), custom_call_target="tpu_custom_call" | custom-call | flops 8556380160 | bytes 8388608 | tf_op jit(solution)/shard_map/shared_prompt_attention/pallas_call | solution.py:426
  50.3 2.4 %hand_over.1 = (bf16[128,2560]{1,0:T(8,128)(2,1)}, bf16[128,2560]{1,0:T(8,128)(2,1)}, bf16[128,2,512]{2,1,0:T(2,128)(2,1)}, bf16[128,2,512]{2,1,0:T(2,128)(2,1)}) custom-call(bf16[128,2560]{1,0:T(8,128)(2,1)} %get-tuple-element.8.refs_0_, bf16[128,2560]{1,0:T(8,128)(2,1)} %get-tuple-element.9.refs_1_, bf16[128,2,512]{2,1,0:T(2,128)(2,1)} %get-tuple-element.10.refs_2_, ...), custom_call_target="tpu_custom_call" | custom-call | tf_op jit(solution)/shard_map/hand_over/pallas_call | solution.py:476

commit v5 on v4

--- a/solution.py
+++ b/solution.py
@@ -259,7 +259,7 @@
         for b in (0, 1):
             s = dot(xr[a, b, 0], stacked(xq, a, b), 1, 1)
             srb[a, :, b * COLS:(b + 1) * COLS] = jnp.where(key <= slot, s, MASKED)
-        mb[a] = fold(srb[a], jnp.max)
+        mb[a] = jnp.maximum(mb[a], fold(srb[a], jnp.max))
 
     def own_weights(a):
         tp[a] = jnp.max(mb[a], axis=0, keepdims=True)
@@ -347,12 +347,14 @@
     def near_ends(a):
         return {0: [f(sum_three, a), f(sum_two, a)], 1: [f(sum_one, a), rs_last(a, 0, 1).start]}
 
-    for pair in (ex_q, ex_r, ex_kv):
-        exchange_wait(pair)
+    exchange_wait(ex_q)
+    exchange_wait(ex_kv)
     for a in (0, 1):
         dqt[a] = jnp.zeros((D, R), F32)
+        mb[a] = jnp.full((8, R), MASKED, F32)
+    loop({0: [f(ag_second, 0, 0)]}, [scores(0, 0)])
+    exchange_wait(ex_r)
     own_scores(0)
-    loop({0: [f(ag_second, 0, 0)]}, [scores(0, 0)])
     own_weights(0)
     own_scores(1)
     loop({0: [f(ag_second, 0, 1), f(ag_second, 1, 0)]}, [weigh(0, 0), scores(1, 0)])

time: 53 us -> 53 us (level)
  no operation moved by 1% of the time
where the time goes in v5:
time: 53 us; the launch traced here: 52.8 us
  Pallas kernels  51.4 us (97%)
  between operations  1.45 us (3%)
    pallas_call x1, Pallas kernels, per_device(): pl.pallas_call(kernel, out_shape=(jax.ShapeDtypeStruct(queries.shape, BF)...  49 us
    pallas_call x1, Pallas kernels, per_device(): pl.pallas_call(hand_over, out_shape=tuple((jax.ShapeDtypeStruct(v.shape,...  2.38 us

profile of v5, /device:TPU:1, one launch (start us, length us, event | category | flops | bytes accessed | tf_op | source)
XLA Modules:
  0.0 52.8 jit_solution(11653061622192822149)
XLA Ops:
  1.3 49.0 %shared_prompt_attention.1 = (bf16[128,2560]{1,0:T(8,128)(2,1)}, bf16[128,2560]{1,0:T(8,128)(2,1)}, bf16[128,2,512]{2,1,0:T(2,128)(2,1)}, bf16[128,2,512]{2,1,0:T(2,128)(2,1)}) custom-call(s32[1]{0:T(128)S(6)} %copy.9.lengths, bf16[128,2,512]{2,1,0:T(2,128)(2,1)} %prompt.1, bf16[128,2,512]{2,1,0:T(2,128)(2,1)} %resp.1, bf16[128,2560]{1,0:T(8,128)(2,1)} %query.1, ...), custom_call_target="tpu_custom_call" | custom-call | flops 8556380160 | bytes 8388608 | tf_op jit(solution)/shard_map/shared_prompt_attention/pallas_call | solution.py:428
  50.3 2.4 %hand_over.1 = (bf16[128,2560]{1,0:T(8,128)(2,1)}, bf16[128,2560]{1,0:T(8,128)(2,1)}, bf16[128,2,512]{2,1,0:T(2,128)(2,1)}, bf16[128,2,512]{2,1,0:T(2,128)(2,1)}) custom-call(bf16[128,2560]{1,0:T(8,128)(2,1)} %get-tuple-element.8.refs_0_, bf16[128,2560]{1,0:T(8,128)(2,1)} %get-tuple-element.9.refs_1_, bf16[128,2,512]{2,1,0:T(2,128)(2,1)} %get-tuple-element.10.refs_2_, ...), custom_call_target="tpu_custom_call" | custom-call | tf_op jit(solution)/shard_map/hand_over/pallas_call | solution.py:478
